TPU v7x, 32 devices: a whole 2x2x4 slice. The times are simulated.
32 devices in a mesh: span: 4 (over y, x), tm: 8 (over z, core).
Axes of the slice: x: 2, y: 2, z: 4, core: 2. Of those that a mesh axis runs over, the one named last changes fastest.
Arguments:
- launched: float32 [8, 2, 110, 2048], P(None, None, None, 'tm'), may hold values from -1.5 to 1.5
- coupling: float32 [4, 2, 2, 2, 110, 110], P('span'), may hold values from -2 to 2
- impulse: float32 [4, 2, 2, 2, 129], P('span'), may hold values from -1.5 to 1.5
- amplifier: float32 [4, 2, 110], P('span'), may hold values from 0.9 to 1.11
- nonlinear: float32 [4, 2, 2], P('span'), may hold values from 0.002 to 0.008
Outputs:
- monitored: float32 [4, 8, 2, 110, 2048], P('span', None, None, None, 'tm')
All inputs are finite; a program needn't handle non-finite values.
Results may differ from a plain program's by a relative error of at most 0.0004.
Values sent between devices are 32-bit elements; how exact they have to be, the bound alone decides.
A program may use at most 64 MiB of HBM per device.

v0:
```python
import jax
import jax.numpy as jnp
from jax import lax
from jax.sharding import PartitionSpec as P


def padded_2(block, sides, width):
    for axis, dim in sides:
        count = lax.axis_size(axis)
        forward = [(i, i + 1) for i in range(count - 1)]
        backward = [(target, source) for source, target in forward]
        low = lax.ppermute(
            lax.slice_in_dim(block, block.shape[dim] - width, None, axis=dim), axis, forward
        )
        high = lax.ppermute(lax.slice_in_dim(block, 0, width, axis=dim), axis, backward)
        block = jnp.concatenate([low, block, high], axis=dim)
    return block


def passed_along(value, axis, by):
    length = lax.axis_size(axis)
    pairs = [(i, i + by) for i in range(length) if 0 <= i + by < length]
    return lax.ppermute(value, axis, pairs)


def band(values, width):
    padded = jnp.concatenate([values, jnp.zeros((width,), jnp.float32)])
    tiled = jnp.tile(padded, width)[: width * 2 * width]
    return tiled.reshape(width, 2 * width).T


def prepare(coupling_group, impulse_group):
    half_taps = (impulse_group.shape[-1] - 1) // 2
    width = 2 * half_taps

    def toeplitz(pair):
        real_band = band(pair[0], width)
        imag_band = band(pair[1], width)
        upper = jnp.concatenate([real_band, imag_band], axis=1)
        lower = jnp.concatenate([-imag_band, real_band], axis=1)
        return jnp.concatenate([upper, lower], axis=0)

    filters = jax.vmap(jax.vmap(toeplitz))(impulse_group)
    real_part = coupling_group[:, :, 0]
    imag_part = coupling_group[:, :, 1]
    upper = jnp.concatenate([real_part, -imag_part], axis=-1)
    lower = jnp.concatenate([imag_part, real_part], axis=-1)
    return (filters, jnp.concatenate([upper, lower], axis=-2))


def disperse(extended, matrix, half_taps):
    width = 2 * half_taps
    frames, _, channels, extent = extended.shape
    block_count = extent // width - 1
    blocks = extended.reshape(frames, 2, channels, block_count + 1, width)
    windows = jnp.concatenate([blocks[..., :-1, :], blocks[..., 1:, :]], axis=-1)
    stacked = jnp.concatenate([windows[:, 0], windows[:, 1]], axis=-1)
    product = jnp.einsum("fcbu,uv->fcbv", stacked, matrix, precision=lax.Precision.HIGHEST)
    real_part = product[..., :width].reshape(frames, channels, block_count * width)
    imag_part = product[..., width:].reshape(frames, channels, block_count * width)
    return jnp.stack([real_part, imag_part], axis=1)


def couple(signal, mixer, coefficient):
    frames, _, channels, extent = signal.shape
    flat = signal.reshape(frames, 2 * channels, extent)
    mixed = jnp.einsum("de,fel->fdl", mixer, flat, precision=lax.Precision.HIGHEST).reshape(
        frames, 2, channels, extent
    )
    power = jnp.sum(mixed * mixed, axis=(1, 2))
    phase = coefficient * power[:, None, :]
    cosine = jnp.cos(phase)
    sine = jnp.sin(phase)
    real_part = mixed[:, 0]
    imag_part = mixed[:, 1]
    return jnp.stack(
        [real_part * cosine - imag_part * sine, real_part * sine + imag_part * cosine], axis=1
    )


def inside_frame(signal, margin, samples):
    extent = signal.shape[-1]
    positions = lax.axis_index("tm") * samples - margin + jnp.arange(extent, dtype=jnp.int32)
    usable = (positions >= 0) & (positions < samples * lax.axis_size("tm"))
    return signal * usable.astype(jnp.float32)[None, None, None, :]


def propagate(signal, filters, mixers, amplifier_group, nonlinear_group):
    span_count, step_count = nonlinear_group.shape
    half_taps = filters.shape[-1] // 4
    samples = signal.shape[-1]
    margin = 0
    for span_index in range(span_count):
        for step_index in range(step_count):
            if margin == 0:
                signal = padded_2(signal, (("tm", 3),), step_count * half_taps)
                margin = step_count * half_taps
            signal = disperse(signal, filters[span_index, step_index], half_taps)
            margin = margin - half_taps
            if margin > 0:
                signal = inside_frame(signal, margin, samples)
            signal = couple(
                signal, mixers[span_index, step_index], nonlinear_group[span_index, step_index]
            )
        signal = signal * amplifier_group[span_index][None, None, :, None]
    return signal


def shards(launched, coupling, impulse, amplifier, nonlinear):
    frames_count = launched.shape[0]
    sections = lax.axis_size("span")
    section_index = lax.axis_index("span")
    filters, mixers = prepare(coupling[0], impulse[0])
    amplifier_group = amplifier[0]
    nonlinear_group = nonlinear[0]

    def advance(carry, moment):
        received, stored = carry
        source = lax.dynamic_index_in_dim(
            launched, jnp.minimum(moment, frames_count - 1), 0, keepdims=True
        )
        incoming = jnp.where(section_index == 0, source, received)
        result = propagate(incoming, filters, mixers, amplifier_group, nonlinear_group)
        frame_slot = moment - section_index
        usable = (frame_slot >= 0) & (frame_slot < frames_count)
        position = jnp.clip(frame_slot, 0, frames_count - 1)
        previous = lax.dynamic_index_in_dim(stored, position, 0, keepdims=True)
        stored = lax.dynamic_update_index_in_dim(
            stored, jnp.where(usable, result, previous), position, 0
        )
        passed = passed_along(result, "span", 1)
        return ((passed, stored), None)

    start = (jnp.zeros_like(launched[:1]), jnp.zeros_like(launched))
    moments = jnp.arange(frames_count + sections - 1, dtype=jnp.int32)
    (_, stored), _ = lax.scan(advance, start, moments)
    return stored[None]


def solution(mesh):
    placed = (
        P(None, None, None, "tm"),
        P("span", None, None, None, None, None),
        P("span", None, None, None, None),
        P("span", None, None),
        P("span", None, None),
    )
    return jax.shard_map(
        shards,
        mesh=mesh,
        in_specs=placed,
        out_specs=P("span", None, None, None, "tm"),
        check_vma=False,
    )
```

profile of v0, /device:TPU:23, one launch (start us, length us, event | category | flops | bytes accessed | tf_op | source)
XLA Modules:
  0.0 501.5 jit_solution(10217975505448967441)
XLA Ops:
  6.1 1.6 maximum_maximum_fusion
  7.8 1.9 copy.33
  9.7 1.7 broadcast_in_dim.7.clone
  11.4 490.1 %while.14 = (s32[]{:T(128)}, f32[1,2,110,256]{3,2,1,0:T(8,128)S(1)}, f32[8,2,110,256]{3,1,2,0:T(2,128)}, pred[]{:T(512)}, s32[11]{0:T(128)S(1)}, /*index=5*/f32[...) while((s32[]{:T(128)}, ...), condition=%wide.region_5.6_spmd, body=%wide.region_0.5_spmd.sunk | while | flops 2477349888 | bytes 50202268 | solution.py:136
  14.6 2.6 collective-permute-start
  17.2 3.1 collective-permute-start.1
  30.5 3.1 collective-permute-start.2
  33.6 3.1 collective-permute-start.3
  49.1 5.6 %collective-permute-done.4 = f32[1,2,110,256]{3,2,1,0:T(8,128)S(1)} collective-permute-done((f32[1,2,110,256]{3,2,1,0:T(8,128)S(1)}, f32[1,2,110,256]{3,2,1,0:T(8,128)S(1)}, u32[]{:S(2)}, u32[]{:S(2)}) %collective-permute-start.4) | collective-permute-done | bytes 225312 | tf_op jit(solution)/shard_map/while/body/eval_jaxpr/ppermute | solution.py:23
  57.8 4.1 collective-permute-start
  61.9 2.4 collective-permute-start.1
  74.4 3.9 collective-permute-start.2
  78.3 2.3 collective-permute-start.3
  93.0 4.6 collective-permute-done.4
  100.8 5.1 %collective-permute-start = (f32[1,2,110,128]{3,2,1,0:T(8,128)S(1)}, f32[1,2,110,128]{3,2,1,0:T(8,128)S(1)}, u32[]{:S(2)}, u32[]{:S(2)}) collective-permute-start(f32[1,2,110,128]{3,2,1,0:T(8,128)S(1)} %get-tuple-element.373), channel_id=1, source_target_pairs={{1,0},{2,1},{3,2},{4,3},{5,4},{6,5},{7,6},{9,8},{10,9},{11,10},{12... | collective-permute-start | bytes 337928 | tf_op jit(solution)/shard_map/while/body/eval_jaxpr/ppermute | solution.py:15
  105.8 2.4 collective-permute-start.1
  118.4 3.9 collective-permute-start.2
  122.3 2.4 collective-permute-start.3
  128.3 1.5 multiply_reduce_fusion.10
  137.0 5.7 %collective-permute-done.4 = f32[1,2,110,256]{3,2,1,0:T(8,128)S(1)} collective-permute-done((f32[1,2,110,256]{3,2,1,0:T(8,128)S(1)}, f32[1,2,110,256]{3,2,1,0:T(8,128)S(1)}, u32[]{:S(2)}, u32[]{:S(2)}) %collective-permute-start.4) | collective-permute-done | bytes 225312 | tf_op jit(solution)/shard_map/while/body/eval_jaxpr/ppermute | solution.py:23
  145.8 4.5 collective-permute-start
  150.4 2.1 collective-permute-start.1
  162.6 4.2 collective-permute-start.2
  166.8 2.1 collective-permute-start.3
  172.6 1.5 multiply_reduce_fusion.10
  181.3 6.3 %collective-permute-done.4 = f32[1,2,110,256]{3,2,1,0:T(8,128)S(1)} collective-permute-done((f32[1,2,110,256]{3,2,1,0:T(8,128)S(1)}, f32[1,2,110,256]{3,2,1,0:T(8,128)S(1)}, u32[]{:S(2)}, u32[]{:S(2)}) %collective-permute-start.4) | collective-permute-done | bytes 225312 | tf_op jit(solution)/shard_map/while/body/eval_jaxpr/ppermute | solution.py:23
  190.7 4.6 collective-permute-start
  195.2 2.1 collective-permute-start.1
  207.5 4.2 collective-permute-start.2
  211.7 2.1 collective-permute-start.3
  226.1 6.3 %collective-permute-done.4 = f32[1,2,110,256]{3,2,1,0:T(8,128)S(1)} collective-permute-done((f32[1,2,110,256]{3,2,1,0:T(8,128)S(1)}, f32[1,2,110,256]{3,2,1,0:T(8,128)S(1)}, u32[]{:S(2)}, u32[]{:S(2)}) %collective-permute-start.4) | collective-permute-done | bytes 225312 | tf_op jit(solution)/shard_map/while/body/eval_jaxpr/ppermute | solution.py:23
  235.5 4.5 collective-permute-start
  240.1 2.1 collective-permute-start.1
  252.3 4.2 collective-permute-start.2
  256.5 2.1 collective-permute-start.3
  262.3 1.5 multiply_reduce_fusion.10
  271.0 6.3 %collective-permute-done.4 = f32[1,2,110,256]{3,2,1,0:T(8,128)S(1)} collective-permute-done((f32[1,2,110,256]{3,2,1,0:T(8,128)S(1)}, f32[1,2,110,256]{3,2,1,0:T(8,128)S(1)}, u32[]{:S(2)}, u32[]{:S(2)}) %collective-permute-start.4) | collective-permute-done | bytes 225312 | tf_op jit(solution)/shard_map/while/body/eval_jaxpr/ppermute | solution.py:23
  280.4 4.5 collective-permute-start
  284.9 2.1 collective-permute-start.1
  297.2 4.2 collective-permute-start.2
  301.4 2.1 collective-permute-start.3
  307.2 1.5 multiply_reduce_fusion.10
  315.8 6.3 %collective-permute-done.4 = f32[1,2,110,256]{3,2,1,0:T(8,128)S(1)} collective-permute-done((f32[1,2,110,256]{3,2,1,0:T(8,128)S(1)}, f32[1,2,110,256]{3,2,1,0:T(8,128)S(1)}, u32[]{:S(2)}, u32[]{:S(2)}) %collective-permute-start.4) | collective-permute-done | bytes 225312 | tf_op jit(solution)/shard_map/while/body/eval_jaxpr/ppermute | solution.py:23
  325.2 4.6 collective-permute-start
  329.8 2.1 collective-permute-start.1
  342.0 4.2 collective-permute-start.2
  346.2 2.1 collective-permute-start.3
  360.7 6.3 %collective-permute-done.4 = f32[1,2,110,256]{3,2,1,0:T(8,128)S(1)} collective-permute-done((f32[1,2,110,256]{3,2,1,0:T(8,128)S(1)}, f32[1,2,110,256]{3,2,1,0:T(8,128)S(1)}, u32[]{:S(2)}, u32[]{:S(2)}) %collective-permute-start.4) | collective-permute-done | bytes 225312 | tf_op jit(solution)/shard_map/while/body/eval_jaxpr/ppermute | solution.py:23
  370.1 4.5 collective-permute-start
  374.6 2.1 collective-permute-start.1
  386.9 4.2 collective-permute-start.2
  391.1 2.1 collective-permute-start.3
  396.9 1.5 multiply_reduce_fusion.10
  405.5 6.3 %collective-permute-done.4 = f32[1,2,110,256]{3,2,1,0:T(8,128)S(1)} collective-permute-done((f32[1,2,110,256]{3,2,1,0:T(8,128)S(1)}, f32[1,2,110,256]{3,2,1,0:T(8,128)S(1)}, u32[]{:S(2)}, u32[]{:S(2)}) %collective-permute-start.4) | collective-permute-done | bytes 225312 | tf_op jit(solution)/shard_map/while/body/eval_jaxpr/ppermute | solution.py:23
  415.0 4.5 collective-permute-start
  419.5 2.1 collective-permute-start.1
  431.8 4.2 collective-permute-start.2
  436.0 2.1 collective-permute-start.3
  450.4 6.3 %collective-permute-done.4 = f32[1,2,110,256]{3,2,1,0:T(8,128)S(1)} collective-permute-done((f32[1,2,110,256]{3,2,1,0:T(8,128)S(1)}, f32[1,2,110,256]{3,2,1,0:T(8,128)S(1)}, u32[]{:S(2)}, u32[]{:S(2)}) %collective-permute-start.4) | collective-permute-done | bytes 225312 | tf_op jit(solution)/shard_map/while/body/eval_jaxpr/ppermute | solution.py:23
  459.8 4.6 collective-permute-start
  464.4 2.1 collective-permute-start.1
  476.6 4.2 collective-permute-start.2
  480.8 2.1 collective-permute-start.3
  495.2 6.3 %collective-permute-done.4 = f32[1,2,110,256]{3,2,1,0:T(8,128)S(1)} collective-permute-done((f32[1,2,110,256]{3,2,1,0:T(8,128)S(1)}, f32[1,2,110,256]{3,2,1,0:T(8,128)S(1)}, u32[]{:S(2)}, u32[]{:S(2)}) %collective-permute-start.4) | collective-permute-done | bytes 225312 | tf_op jit(solution)/shard_map/while/body/eval_jaxpr/ppermute | solution.py:23
  (942 shorter events, 261.1 us)
Async XLA Ops:
  7.8 3.7 copy-start
  7.8 3.7 copy-start.1
  14.6 6.4 %collective-permute-start = (f32[1,2,110,128]{3,2,1,0:T(8,128)S(1)}, f32[1,2,110,128]{3,2,1,0:T(8,128)S(1)}, u32[]{:S(2)}, u32[]{:S(2)}) collective-permute-start(f32[1,2,110,128]{3,2,1,0:T(8,128)S(1)} %get-tuple-element.373), channel_id=1, source_target_pairs={{1,0},{2,1},{3,2},{4,3},{5,4},{6,5},{7,6},{9,8},{10,9},{11,10},{12... | collective-permute-start | bytes 337928 | tf_op jit(solution)/shard_map/while/body/eval_jaxpr/ppermute | solution.py:15
  17.2 4.9 collective-permute-start.1
  30.5 6.8 %collective-permute-start.2 = (f32[1,2,110,128]{3,2,1,0:T(8,128)S(1)}, f32[1,2,110,128]{3,2,1,0:T(8,128)S(1)}, u32[]{:S(2)}, u32[]{:S(2)}) collective-permute-start(f32[1,2,110,128]{3,2,1,0:T(8,128)S(1)} %get-tuple-element.400), channel_id=1, source_target_pairs={{1,0},{2,1},{3,2},{4,3},{5,4},{6,5},{7,6},{9,8},{10,9},{11,10},{12... | collective-permute-start | bytes 337928 | tf_op jit(solution)/shard_map/while/body/eval_jaxpr/ppermute | solution.py:15
  33.6 4.9 collective-permute-start.3
  46.9 7.7 %collective-permute-start.4 = (f32[1,2,110,256]{3,2,1,0:T(8,128)S(1)}, f32[1,2,110,256]{3,2,1,0:T(8,128)S(1)}, u32[]{:S(2)}, u32[]{:S(2)}) collective-permute-start(f32[1,2,110,256]{3,2,1,0:T(8,128)S(1)} %get-tuple-element.426), channel_id=1, source_target_pairs={{0,8},{8,16},{16,24},{1,9},{9,17},{17,25},{2,10},{10,18},{18,26},{... | collective-permute-start | bytes 675848 | tf_op jit(solution)/shard_map/while/body/eval_jaxpr/ppermute | solution.py:23
  57.8 7.1 %collective-permute-start = (f32[1,2,110,128]{3,2,1,0:T(8,128)S(1)}, f32[1,2,110,128]{3,2,1,0:T(8,128)S(1)}, u32[]{:S(2)}, u32[]{:S(2)}) collective-permute-start(f32[1,2,110,128]{3,2,1,0:T(8,128)S(1)} %get-tuple-element.373), channel_id=1, source_target_pairs={{1,0},{2,1},{3,2},{4,3},{5,4},{6,5},{7,6},{9,8},{10,9},{11,10},{12... | collective-permute-start | bytes 337928 | tf_op jit(solution)/shard_map/while/body/eval_jaxpr/ppermute | solution.py:15
  61.9 4.1 collective-permute-start.1
  74.4 6.8 %collective-permute-start.2 = (f32[1,2,110,128]{3,2,1,0:T(8,128)S(1)}, f32[1,2,110,128]{3,2,1,0:T(8,128)S(1)}, u32[]{:S(2)}, u32[]{:S(2)}) collective-permute-start(f32[1,2,110,128]{3,2,1,0:T(8,128)S(1)} %get-tuple-element.400), channel_id=1, source_target_pairs={{1,0},{2,1},{3,2},{4,3},{5,4},{6,5},{7,6},{9,8},{10,9},{11,10},{12... | collective-permute-start | bytes 337928 | tf_op jit(solution)/shard_map/while/body/eval_jaxpr/ppermute | solution.py:15
  78.3 4.1 collective-permute-start.3
  90.9 6.8 %collective-permute-start.4 = (f32[1,2,110,256]{3,2,1,0:T(8,128)S(1)}, f32[1,2,110,256]{3,2,1,0:T(8,128)S(1)}, u32[]{:S(2)}, u32[]{:S(2)}) collective-permute-start(f32[1,2,110,256]{3,2,1,0:T(8,128)S(1)} %get-tuple-element.426), channel_id=1, source_target_pairs={{0,8},{8,16},{16,24},{1,9},{9,17},{17,25},{2,10},{10,18},{18,26},{... | collective-permute-start | bytes 675848 | tf_op jit(solution)/shard_map/while/body/eval_jaxpr/ppermute | solution.py:23
  100.8 8.1 %collective-permute-start = (f32[1,2,110,128]{3,2,1,0:T(8,128)S(1)}, f32[1,2,110,128]{3,2,1,0:T(8,128)S(1)}, u32[]{:S(2)}, u32[]{:S(2)}) collective-permute-start(f32[1,2,110,128]{3,2,1,0:T(8,128)S(1)} %get-tuple-element.373), channel_id=1, source_target_pairs={{1,0},{2,1},{3,2},{4,3},{5,4},{6,5},{7,6},{9,8},{10,9},{11,10},{12... | collective-permute-start | bytes 337928 | tf_op jit(solution)/shard_map/while/body/eval_jaxpr/ppermute | solution.py:15
  105.8 4.1 collective-permute-start.1
  118.4 6.8 %collective-permute-start.2 = (f32[1,2,110,128]{3,2,1,0:T(8,128)S(1)}, f32[1,2,110,128]{3,2,1,0:T(8,128)S(1)}, u32[]{:S(2)}, u32[]{:S(2)}) collective-permute-start(f32[1,2,110,128]{3,2,1,0:T(8,128)S(1)} %get-tuple-element.400), channel_id=1, source_target_pairs={{1,0},{2,1},{3,2},{4,3},{5,4},{6,5},{7,6},{9,8},{10,9},{11,10},{12... | collective-permute-start | bytes 337928 | tf_op jit(solution)/shard_map/while/body/eval_jaxpr/ppermute | solution.py:15
  122.3 4.1 collective-permute-start.3
  134.8 7.9 %collective-permute-start.4 = (f32[1,2,110,256]{3,2,1,0:T(8,128)S(1)}, f32[1,2,110,256]{3,2,1,0:T(8,128)S(1)}, u32[]{:S(2)}, u32[]{:S(2)}) collective-permute-start(f32[1,2,110,256]{3,2,1,0:T(8,128)S(1)} %get-tuple-element.426), channel_id=1, source_target_pairs={{0,8},{8,16},{16,24},{1,9},{9,17},{17,25},{2,10},{10,18},{18,26},{... | collective-permute-start | bytes 675848 | tf_op jit(solution)/shard_map/while/body/eval_jaxpr/ppermute | solution.py:23
  145.8 7.3 %collective-permute-start = (f32[1,2,110,128]{3,2,1,0:T(8,128)S(1)}, f32[1,2,110,128]{3,2,1,0:T(8,128)S(1)}, u32[]{:S(2)}, u32[]{:S(2)}) collective-permute-start(f32[1,2,110,128]{3,2,1,0:T(8,128)S(1)} %get-tuple-element.373), channel_id=1, source_target_pairs={{1,0},{2,1},{3,2},{4,3},{5,4},{6,5},{7,6},{9,8},{10,9},{11,10},{12... | collective-permute-start | bytes 337928 | tf_op jit(solution)/shard_map/while/body/eval_jaxpr/ppermute | solution.py:15
  150.4 3.8 collective-permute-start.1
  162.6 6.8 %collective-permute-start.2 = (f32[1,2,110,128]{3,2,1,0:T(8,128)S(1)}, f32[1,2,110,128]{3,2,1,0:T(8,128)S(1)}, u32[]{:S(2)}, u32[]{:S(2)}) collective-permute-start(f32[1,2,110,128]{3,2,1,0:T(8,128)S(1)} %get-tuple-element.400), channel_id=1, source_target_pairs={{1,0},{2,1},{3,2},{4,3},{5,4},{6,5},{7,6},{9,8},{10,9},{11,10},{12... | collective-permute-start | bytes 337928 | tf_op jit(solution)/shard_map/while/body/eval_jaxpr/ppermute | solution.py:15
  166.8 3.8 collective-permute-start.3
  179.1 8.4 %collective-permute-start.4 = (f32[1,2,110,256]{3,2,1,0:T(8,128)S(1)}, f32[1,2,110,256]{3,2,1,0:T(8,128)S(1)}, u32[]{:S(2)}, u32[]{:S(2)}) collective-permute-start(f32[1,2,110,256]{3,2,1,0:T(8,128)S(1)} %get-tuple-element.426), channel_id=1, source_target_pairs={{0,8},{8,16},{16,24},{1,9},{9,17},{17,25},{2,10},{10,18},{18,26},{... | collective-permute-start | bytes 675848 | tf_op jit(solution)/shard_map/while/body/eval_jaxpr/ppermute | solution.py:23
  190.7 7.3 %collective-permute-start = (f32[1,2,110,128]{3,2,1,0:T(8,128)S(1)}, f32[1,2,110,128]{3,2,1,0:T(8,128)S(1)}, u32[]{:S(2)}, u32[]{:S(2)}) collective-permute-start(f32[1,2,110,128]{3,2,1,0:T(8,128)S(1)} %get-tuple-element.373), channel_id=1, source_target_pairs={{1,0},{2,1},{3,2},{4,3},{5,4},{6,5},{7,6},{9,8},{10,9},{11,10},{12... | collective-permute-start | bytes 337928 | tf_op jit(solution)/shard_map/while/body/eval_jaxpr/ppermute | solution.py:15
  195.2 3.8 collective-permute-start.1
  207.5 6.8 %collective-permute-start.2 = (f32[1,2,110,128]{3,2,1,0:T(8,128)S(1)}, f32[1,2,110,128]{3,2,1,0:T(8,128)S(1)}, u32[]{:S(2)}, u32[]{:S(2)}) collective-permute-start(f32[1,2,110,128]{3,2,1,0:T(8,128)S(1)} %get-tuple-element.400), channel_id=1, source_target_pairs={{1,0},{2,1},{3,2},{4,3},{5,4},{6,5},{7,6},{9,8},{10,9},{11,10},{12... | collective-permute-start | bytes 337928 | tf_op jit(solution)/shard_map/while/body/eval_jaxpr/ppermute | solution.py:15
  211.7 3.8 collective-permute-start.3
  223.9 8.5 %collective-permute-start.4 = (f32[1,2,110,256]{3,2,1,0:T(8,128)S(1)}, f32[1,2,110,256]{3,2,1,0:T(8,128)S(1)}, u32[]{:S(2)}, u32[]{:S(2)}) collective-permute-start(f32[1,2,110,256]{3,2,1,0:T(8,128)S(1)} %get-tuple-element.426), channel_id=1, source_target_pairs={{0,8},{8,16},{16,24},{1,9},{9,17},{17,25},{2,10},{10,18},{18,26},{... | collective-permute-start | bytes 675848 | tf_op jit(solution)/shard_map/while/body/eval_jaxpr/ppermute | solution.py:23
  235.5 7.3 %collective-permute-start = (f32[1,2,110,128]{3,2,1,0:T(8,128)S(1)}, f32[1,2,110,128]{3,2,1,0:T(8,128)S(1)}, u32[]{:S(2)}, u32[]{:S(2)}) collective-permute-start(f32[1,2,110,128]{3,2,1,0:T(8,128)S(1)} %get-tuple-element.373), channel_id=1, source_target_pairs={{1,0},{2,1},{3,2},{4,3},{5,4},{6,5},{7,6},{9,8},{10,9},{11,10},{12... | collective-permute-start | bytes 337928 | tf_op jit(solution)/shard_map/while/body/eval_jaxpr/ppermute | solution.py:15
  240.1 3.9 collective-permute-start.1
  252.3 6.8 %collective-permute-start.2 = (f32[1,2,110,128]{3,2,1,0:T(8,128)S(1)}, f32[1,2,110,128]{3,2,1,0:T(8,128)S(1)}, u32[]{:S(2)}, u32[]{:S(2)}) collective-permute-start(f32[1,2,110,128]{3,2,1,0:T(8,128)S(1)} %get-tuple-element.400), channel_id=1, source_target_pairs={{1,0},{2,1},{3,2},{4,3},{5,4},{6,5},{7,6},{9,8},{10,9},{11,10},{12... | collective-permute-start | bytes 337928 | tf_op jit(solution)/shard_map/while/body/eval_jaxpr/ppermute | solution.py:15
  256.5 3.9 collective-permute-start.3
  268.8 8.5 %collective-permute-start.4 = (f32[1,2,110,256]{3,2,1,0:T(8,128)S(1)}, f32[1,2,110,256]{3,2,1,0:T(8,128)S(1)}, u32[]{:S(2)}, u32[]{:S(2)}) collective-permute-start(f32[1,2,110,256]{3,2,1,0:T(8,128)S(1)} %get-tuple-element.426), channel_id=1, source_target_pairs={{0,8},{8,16},{16,24},{1,9},{9,17},{17,25},{2,10},{10,18},{18,26},{... | collective-permute-start | bytes 675848 | tf_op jit(solution)/shard_map/while/body/eval_jaxpr/ppermute | solution.py:23
  280.4 7.3 %collective-permute-start = (f32[1,2,110,128]{3,2,1,0:T(8,128)S(1)}, f32[1,2,110,128]{3,2,1,0:T(8,128)S(1)}, u32[]{:S(2)}, u32[]{:S(2)}) collective-permute-start(f32[1,2,110,128]{3,2,1,0:T(8,128)S(1)} %get-tuple-element.373), channel_id=1, source_target_pairs={{1,0},{2,1},{3,2},{4,3},{5,4},{6,5},{7,6},{9,8},{10,9},{11,10},{12... | collective-permute-start | bytes 337928 | tf_op jit(solution)/shard_map/while/body/eval_jaxpr/ppermute | solution.py:15
  284.9 3.8 collective-permute-start.1
  297.2 6.8 %collective-permute-start.2 = (f32[1,2,110,128]{3,2,1,0:T(8,128)S(1)}, f32[1,2,110,128]{3,2,1,0:T(8,128)S(1)}, u32[]{:S(2)}, u32[]{:S(2)}) collective-permute-start(f32[1,2,110,128]{3,2,1,0:T(8,128)S(1)} %get-tuple-element.400), channel_id=1, source_target_pairs={{1,0},{2,1},{3,2},{4,3},{5,4},{6,5},{7,6},{9,8},{10,9},{11,10},{12... | collective-permute-start | bytes 337928 | tf_op jit(solution)/shard_map/while/body/eval_jaxpr/ppermute | solution.py:15
  301.4 3.8 collective-permute-start.3
  313.6 8.4 %collective-permute-start.4 = (f32[1,2,110,256]{3,2,1,0:T(8,128)S(1)}, f32[1,2,110,256]{3,2,1,0:T(8,128)S(1)}, u32[]{:S(2)}, u32[]{:S(2)}) collective-permute-start(f32[1,2,110,256]{3,2,1,0:T(8,128)S(1)} %get-tuple-element.426), channel_id=1, source_target_pairs={{0,8},{8,16},{16,24},{1,9},{9,17},{17,25},{2,10},{10,18},{18,26},{... | collective-permute-start | bytes 675848 | tf_op jit(solution)/shard_map/while/body/eval_jaxpr/ppermute | solution.py:23
  325.2 7.3 %collective-permute-start = (f32[1,2,110,128]{3,2,1,0:T(8,128)S(1)}, f32[1,2,110,128]{3,2,1,0:T(8,128)S(1)}, u32[]{:S(2)}, u32[]{:S(2)}) collective-permute-start(f32[1,2,110,128]{3,2,1,0:T(8,128)S(1)} %get-tuple-element.373), channel_id=1, source_target_pairs={{1,0},{2,1},{3,2},{4,3},{5,4},{6,5},{7,6},{9,8},{10,9},{11,10},{12... | collective-permute-start | bytes 337928 | tf_op jit(solution)/shard_map/while/body/eval_jaxpr/ppermute | solution.py:15
  329.8 3.8 collective-permute-start.1
  342.0 6.8 %collective-permute-start.2 = (f32[1,2,110,128]{3,2,1,0:T(8,128)S(1)}, f32[1,2,110,128]{3,2,1,0:T(8,128)S(1)}, u32[]{:S(2)}, u32[]{:S(2)}) collective-permute-start(f32[1,2,110,128]{3,2,1,0:T(8,128)S(1)} %get-tuple-element.400), channel_id=1, source_target_pairs={{1,0},{2,1},{3,2},{4,3},{5,4},{6,5},{7,6},{9,8},{10,9},{11,10},{12... | collective-permute-start | bytes 337928 | tf_op jit(solution)/shard_map/while/body/eval_jaxpr/ppermute | solution.py:15
  346.2 3.8 collective-permute-start.3
  358.5 8.5 %collective-permute-start.4 = (f32[1,2,110,256]{3,2,1,0:T(8,128)S(1)}, f32[1,2,110,256]{3,2,1,0:T(8,128)S(1)}, u32[]{:S(2)}, u32[]{:S(2)}) collective-permute-start(f32[1,2,110,256]{3,2,1,0:T(8,128)S(1)} %get-tuple-element.426), channel_id=1, source_target_pairs={{0,8},{8,16},{16,24},{1,9},{9,17},{17,25},{2,10},{10,18},{18,26},{... | collective-permute-start | bytes 675848 | tf_op jit(solution)/shard_map/while/body/eval_jaxpr/ppermute | solution.py:23
  370.1 7.3 %collective-permute-start = (f32[1,2,110,128]{3,2,1,0:T(8,128)S(1)}, f32[1,2,110,128]{3,2,1,0:T(8,128)S(1)}, u32[]{:S(2)}, u32[]{:S(2)}) collective-permute-start(f32[1,2,110,128]{3,2,1,0:T(8,128)S(1)} %get-tuple-element.373), channel_id=1, source_target_pairs={{1,0},{2,1},{3,2},{4,3},{5,4},{6,5},{7,6},{9,8},{10,9},{11,10},{12... | collective-permute-start | bytes 337928 | tf_op jit(solution)/shard_map/while/body/eval_jaxpr/ppermute | solution.py:15
  374.6 3.9 collective-permute-start.1
  386.9 6.8 %collective-permute-start.2 = (f32[1,2,110,128]{3,2,1,0:T(8,128)S(1)}, f32[1,2,110,128]{3,2,1,0:T(8,128)S(1)}, u32[]{:S(2)}, u32[]{:S(2)}) collective-permute-start(f32[1,2,110,128]{3,2,1,0:T(8,128)S(1)} %get-tuple-element.400), channel_id=1, source_target_pairs={{1,0},{2,1},{3,2},{4,3},{5,4},{6,5},{7,6},{9,8},{10,9},{11,10},{12... | collective-permute-start | bytes 337928 | tf_op jit(solution)/shard_map/while/body/eval_jaxpr/ppermute | solution.py:15
  391.1 3.9 collective-permute-start.3
  403.4 8.5 %collective-permute-start.4 = (f32[1,2,110,256]{3,2,1,0:T(8,128)S(1)}, f32[1,2,110,256]{3,2,1,0:T(8,128)S(1)}, u32[]{:S(2)}, u32[]{:S(2)}) collective-permute-start(f32[1,2,110,256]{3,2,1,0:T(8,128)S(1)} %get-tuple-element.426), channel_id=1, source_target_pairs={{0,8},{8,16},{16,24},{1,9},{9,17},{17,25},{2,10},{10,18},{18,26},{... | collective-permute-start | bytes 675848 | tf_op jit(solution)/shard_map/while/body/eval_jaxpr/ppermute | solution.py:23
  415.0 7.3 %collective-permute-start = (f32[1,2,110,128]{3,2,1,0:T(8,128)S(1)}, f32[1,2,110,128]{3,2,1,0:T(8,128)S(1)}, u32[]{:S(2)}, u32[]{:S(2)}) collective-permute-start(f32[1,2,110,128]{3,2,1,0:T(8,128)S(1)} %get-tuple-element.373), channel_id=1, source_target_pairs={{1,0},{2,1},{3,2},{4,3},{5,4},{6,5},{7,6},{9,8},{10,9},{11,10},{12... | collective-permute-start | bytes 337928 | tf_op jit(solution)/shard_map/while/body/eval_jaxpr/ppermute | solution.py:15
  419.5 3.8 collective-permute-start.1
  431.8 6.8 %collective-permute-start.2 = (f32[1,2,110,128]{3,2,1,0:T(8,128)S(1)}, f32[1,2,110,128]{3,2,1,0:T(8,128)S(1)}, u32[]{:S(2)}, u32[]{:S(2)}) collective-permute-start(f32[1,2,110,128]{3,2,1,0:T(8,128)S(1)} %get-tuple-element.400), channel_id=1, source_target_pairs={{1,0},{2,1},{3,2},{4,3},{5,4},{6,5},{7,6},{9,8},{10,9},{11,10},{12... | collective-permute-start | bytes 337928 | tf_op jit(solution)/shard_map/while/body/eval_jaxpr/ppermute | solution.py:15
  436.0 3.8 collective-permute-start.3
  448.2 8.4 %collective-permute-start.4 = (f32[1,2,110,256]{3,2,1,0:T(8,128)S(1)}, f32[1,2,110,256]{3,2,1,0:T(8,128)S(1)}, u32[]{:S(2)}, u32[]{:S(2)}) collective-permute-start(f32[1,2,110,256]{3,2,1,0:T(8,128)S(1)} %get-tuple-element.426), channel_id=1, source_target_pairs={{0,8},{8,16},{16,24},{1,9},{9,17},{17,25},{2,10},{10,18},{18,26},{... | collective-permute-start | bytes 675848 | tf_op jit(solution)/shard_map/while/body/eval_jaxpr/ppermute | solution.py:23
  459.8 7.3 %collective-permute-start = (f32[1,2,110,128]{3,2,1,0:T(8,128)S(1)}, f32[1,2,110,128]{3,2,1,0:T(8,128)S(1)}, u32[]{:S(2)}, u32[]{:S(2)}) collective-permute-start(f32[1,2,110,128]{3,2,1,0:T(8,128)S(1)} %get-tuple-element.373), channel_id=1, source_target_pairs={{1,0},{2,1},{3,2},{4,3},{5,4},{6,5},{7,6},{9,8},{10,9},{11,10},{12... | collective-permute-start | bytes 337928 | tf_op jit(solution)/shard_map/while/body/eval_jaxpr/ppermute | solution.py:15
  464.4 3.8 collective-permute-start.1
  476.6 6.8 %collective-permute-start.2 = (f32[1,2,110,128]{3,2,1,0:T(8,128)S(1)}, f32[1,2,110,128]{3,2,1,0:T(8,128)S(1)}, u32[]{:S(2)}, u32[]{:S(2)}) collective-permute-start(f32[1,2,110,128]{3,2,1,0:T(8,128)S(1)} %get-tuple-element.400), channel_id=1, source_target_pairs={{1,0},{2,1},{3,2},{4,3},{5,4},{6,5},{7,6},{9,8},{10,9},{11,10},{12... | collective-permute-start | bytes 337928 | tf_op jit(solution)/shard_map/while/body/eval_jaxpr/ppermute | solution.py:15
  480.8 3.8 collective-permute-start.3
  493.1 8.5 %collective-permute-start.4 = (f32[1,2,110,256]{3,2,1,0:T(8,128)S(1)}, f32[1,2,110,256]{3,2,1,0:T(8,128)S(1)}, u32[]{:S(2)}, u32[]{:S(2)}) collective-permute-start(f32[1,2,110,256]{3,2,1,0:T(8,128)S(1)} %get-tuple-element.426), channel_id=1, source_target_pairs={{0,8},{8,16},{16,24},{1,9},{9,17},{17,25},{2,10},{10,18},{18,26},{... | collective-permute-start | bytes 675848 | tf_op jit(solution)/shard_map/while/body/eval_jaxpr/ppermute | solution.py:23
where the time goes:
time: 510 us; the launch traced here: 502 us
  starting transfers between devices  155 us (30%)
  waiting for transfers between devices  97.5 us (19%)
  matrix products  90.4 us (18%)
  local copies, waits for them, and re-layouts  83.9 us (16%)
  other arithmetic  54.1 us (11%)
  loops' own time  20 us (4%)
    ppermute x22, starting transfers between devices, padded_2(): lax.ppermute(lax.slice_in_dim(block, 0, width, axis=dim), axis, backward)  92.5 us
    ppermute x11, waiting for transfers between devices, passed_along(): return lax.ppermute(value, axis, pairs)  66.2 us
    dot_general x44, matrix products, couple(): jnp.einsum('de,fel->fdl', mixer, flat, precision=lax.Precision.HIGHEST)  62.6 us
    ppermute x22, starting transfers between devices, padded_2(): lax.ppermute(lax.slice_in_dim(block, block.shape[dim] - width, None, axis...  48.7 us
    cos x44, other arithmetic, couple(): cosine = jnp.cos(phase)  29.2 us
    dot_general x44, matrix products, disperse(): jnp.einsum('fcbu,uv->fcbv', stacked, matrix, precision=lax.Precision.HIGH...  27.9 us
    ppermute x22, waiting for transfers between devices, padded_2(): lax.ppermute(lax.slice_in_dim(block, block.shape[dim] - width, None, axis...  25.5 us
    another operation x1, loops' own time, shards(): (_, stored), _ = lax.scan(advance, start, moments)  20 us
  transfers between devices with their start and end apart: 55, of which 44 were waited for; matrix products, arithmetic and copies ran while one was open for 3% of the time, Pallas kernels for 0%

commit v1 on v0

v1 whole, which is shorter than its diff:
```python
import functools

import jax
import jax.numpy as jnp
from jax import lax
from jax.experimental import pallas as pl
from jax.experimental.pallas import tpu as pltpu
from jax.sharding import PartitionSpec as P

MESH = pl.DeviceIdType.MESH
LANES = 128


def padded_rows(channels):
    return (channels + 15) // 16 * 16


def halves(value):
    high = value.astype(jnp.bfloat16)
    low = (value - high.astype(jnp.float32)).astype(jnp.bfloat16)
    return high, low


def product(a_high, a_low, b_high, b_low):
    def dot(a, b):
        return jnp.dot(a, b, preferred_element_type=jnp.float32)

    return dot(a_high, b_high) + dot(a_low, b_high) + dot(a_high, b_low)


def cos_sin(angle):
    turns = jnp.floor(angle * 0.6366197723675814 + 0.5)
    r = angle - turns * 1.5703125
    r = r - turns * 4.837512969970703e-4
    r = r - turns * 7.549789948768648e-8
    z = r * r
    sine = r + r * z * (-1.6666654611e-1 + z * (8.3321608736e-3 - z * 1.9515295891e-4))
    cosine = 1.0 - 0.5 * z + z * z * (
        4.166664568298827e-2 + z * (-1.388731625493765e-3 + z * 2.443315711809948e-5)
    )
    quadrant = turns - 4.0 * jnp.floor(turns * 0.25)
    odd = (quadrant == 1.0) | (quadrant == 3.0)
    cos_sign = jnp.where((quadrant == 1.0) | (quadrant == 2.0), -1.0, 1.0)
    sin_sign = jnp.where(quadrant >= 2.0, -1.0, 1.0)
    return cos_sign * jnp.where(odd, sine, cosine), sin_sign * jnp.where(odd, cosine, sine)


def kernel(
    sizes,
    launched_ref,
    pack_ref,
    out_ref,
    lstage,
    own,
    low_halo,
    high_halo,
    packs,
    mix_high,
    mix_low,
    fir_high,
    fir_low,
    ostage,
    lsem,
    psem,
    pack_send,
    pack_recv,
    up_send,
    up_recv,
    down_send,
    down_recv,
    out_send,
    out_recv,
):
    n_span, n_tm, spans, steps, channels, samples, per, edge = sizes
    rows = padded_rows(channels)
    rounds = n_span * spans
    me = lax.axis_index("span")
    tm = lax.axis_index("tm")
    above = jnp.minimum(tm + 1, n_tm - 1)
    below = jnp.maximum(tm - 1, 0)
    has_below = tm > 0
    has_above = tm < n_tm - 1

    def load(f):
        return pltpu.make_async_copy(launched_ref.at[me * per + f], lstage.at[f], lsem.at[f])

    def own_pack(r):
        return pltpu.make_async_copy(pack_ref.at[r], packs.at[me, r], psem.at[r])

    def give_pack(r, by):
        return pltpu.make_async_remote_copy(
            src_ref=pack_ref.at[r],
            dst_ref=packs.at[me, r],
            send_sem=pack_send.at[r, by],
            recv_sem=pack_recv.at[me, r],
            device_id={"span": lax.rem(me + by, n_span)},
            device_id_type=MESH,
        )

    def got_pack(g, r):
        return pltpu.make_async_remote_copy(
            src_ref=pack_ref.at[r],
            dst_ref=packs.at[g, r],
            send_sem=pack_send.at[r, 1],
            recv_sem=pack_recv.at[g, r],
            device_id={"span": g},
            device_id_type=MESH,
        )

    def go_up(t, f):
        return pltpu.make_async_remote_copy(
            src_ref=own.at[t, f, :, pl.ds(samples - edge, edge)],
            dst_ref=low_halo.at[t, f],
            send_sem=up_send.at[t, f],
            recv_sem=up_recv.at[t, f],
            device_id={"tm": above},
            device_id_type=MESH,
        )

    def go_down(t, f):
        return pltpu.make_async_remote_copy(
            src_ref=own.at[t, f, :, pl.ds(0, edge)],
            dst_ref=high_halo.at[t, f],
            send_sem=down_send.at[t, f],
            recv_sem=down_recv.at[t, f],
            device_id={"tm": below},
            device_id_type=MESH,
        )

    def send_edges(t, f):
        @pl.when(has_above)
        def _():
            go_up(t, f).start()

        @pl.when(has_below)
        def _():
            go_down(t, f).start()

    def keep_out(g, f):
        return pltpu.make_async_copy(
            ostage.at[g, f], out_ref.at[0, me * per + f], out_send.at[g, f]
        )

    def send_out(g, f):
        return pltpu.make_async_remote_copy(
            src_ref=ostage.at[g, f],
            dst_ref=out_ref.at[0, me * per + f],
            send_sem=out_send.at[g, f],
            recv_sem=out_recv.at[me, f],
            device_id={"span": g},
            device_id_type=MESH,
        )

    def got_out(source, f):
        return pltpu.make_async_remote_copy(
            src_ref=ostage.at[0, f],
            dst_ref=out_ref.at[0, source * per + f],
            send_sem=out_send.at[0, f],
            recv_sem=out_recv.at[source, f],
            device_id={"span": source},
            device_id_type=MESH,
        )

    for f in range(per):
        load(f).start()
    for r in range(spans):
        own_pack(r).start()

    barrier = pltpu.get_barrier_semaphore()
    for by in range(1, n_span):
        pl.semaphore_signal(
            barrier, inc=1, device_id={"span": lax.rem(me + by, n_span)}, device_id_type=MESH
        )

    @pl.when(has_above)
    def _():
        pl.semaphore_signal(barrier, inc=1, device_id={"tm": above}, device_id_type=MESH)

    @pl.when(has_below)
    def _():
        pl.semaphore_signal(barrier, inc=1, device_id={"tm": below}, device_id_type=MESH)

    for f in range(per):
        load(f).wait()
        for part in range(2):
            own[0, f, pl.ds(part * rows + rows - 8, 8), :] = jnp.zeros((8, samples), jnp.float32)
            own[0, f, pl.ds(part * rows, channels), :] = lstage[f, part]

    pl.semaphore_wait(
        barrier,
        n_span - 1 + jnp.where(has_above, 1, 0) + jnp.where(has_below, 1, 0),
    )
    for r in range(spans):
        for by in range(1, n_span):
            give_pack(r, by).start()
        if r == 0:
            for f in range(per):
                send_edges(0, f)
    for r in range(spans):
        own_pack(r).wait()

    def prepare(t):
        g = t // spans
        r = t % spans

        @pl.when(g != me)
        def _():
            got_pack(g, r).wait_recv()

        for k in range(steps):
            pack = packs[g, r, k]
            real = pack[:rows, :LANES]
            imag = pack[:rows, LANES:]
            mixer = jnp.concatenate(
                [
                    jnp.concatenate([real, -imag], axis=1),
                    jnp.concatenate([imag, real], axis=1),
                ],
                axis=0,
            )
            mix_high[k], mix_low[k] = halves(mixer)
            for part in range(2):
                line = jnp.broadcast_to(pack[rows + part : rows + part + 1], (LANES, 2 * LANES))
                band = pltpu.roll(line, 0, 1, stride=1, stride_axis=0)
                column = pl.ds(part * LANES, LANES)
                high, low = halves(band)
                fir_high[k, pl.ds(0, LANES), column] = high[:, :LANES]
                fir_high[k, pl.ds(LANES, LANES), column] = high[:, LANES:]
                fir_low[k, pl.ds(0, LANES), column] = low[:, :LANES]
                fir_low[k, pl.ds(LANES, LANES), column] = low[:, LANES:]

    gap = jnp.zeros((LANES - rows, 1), jnp.bfloat16)

    def spread(real, imag):
        fill = jnp.broadcast_to(gap, (LANES - rows, real.shape[1]))
        return jnp.concatenate([real, fill, imag, fill], axis=0)

    def advance(t, f):
        g = t // spans
        r = t % spans
        blocks = (
            [low_halo[t, f, :, pl.ds(i, LANES)] for i in range(0, edge, LANES)]
            + [own[t, f, :, pl.ds(i, LANES)] for i in range(0, samples, LANES)]
            + [high_halo[t, f, :, pl.ds(i, LANES)] for i in range(0, edge, LANES)]
        )
        margin = edge
        for k in range(steps):
            margin = margin - edge // steps
            split = [halves(block) for block in blocks]
            count = len(blocks) - 1
            high = jnp.concatenate(
                [
                    jnp.concatenate([split[b][0], split[b + 1][0]], axis=1)
                    for b in range(count)
                ],
                axis=0,
            )
            low = jnp.concatenate(
                [
                    jnp.concatenate([split[b][1], split[b + 1][1]], axis=1)
                    for b in range(count)
                ],
                axis=0,
            )
            wide = product(high, low, fir_high[k], fir_low[k])
            real_parts = []
            imag_parts = []
            for b in range(count):
                top = wide[b * 2 * rows : b * 2 * rows + rows]
                bottom = wide[b * 2 * rows + rows : (b + 1) * 2 * rows]
                real_parts.append(top[:, :LANES] - bottom[:, LANES:])
                imag_parts.append(top[:, LANES:] + bottom[:, :LANES])
            real = jnp.concatenate(real_parts, axis=1)
            imag = jnp.concatenate(imag_parts, axis=1)
            if margin > 0:
                extent = count * LANES
                place = tm * samples - margin + lax.broadcasted_iota(jnp.int32, (1, extent), 1)
                inside = ((place >= 0) & (place < samples * n_tm)).astype(jnp.float32)
                real = real * inside
                imag = imag * inside
            real_high, real_low = halves(real)
            imag_high, imag_low = halves(imag)
            mixed = product(
                mix_high[k],
                mix_low[k],
                spread(real_high, imag_high),
                spread(real_low, imag_low),
            )
            power = jnp.sum(mixed * mixed, axis=0, keepdims=True)
            cosine, sine = cos_sin(power * packs[g, r, k, 0:1, LANES - 2 : LANES - 1])
            real = mixed[:rows] * cosine - mixed[rows:] * sine
            imag = mixed[:rows] * sine + mixed[rows:] * cosine
            if k == steps - 1:
                gain = packs[g, r, k, :rows, LANES - 1 : LANES]
                real = real * gain
                imag = imag * gain
            both = jnp.concatenate([real, imag], axis=0)
            blocks = [both[:, b * LANES : (b + 1) * LANES] for b in range(count)]
        own[t + 1, f] = both

        @pl.when(t + 1 < rounds)
        def _():
            send_edges(t + 1, f)

        @pl.when(r == spans - 1)
        def _():
            ostage[g, f, 0] = real[:channels]
            ostage[g, f, 1] = imag[:channels]

            @pl.when(g == me)
            def _():
                keep_out(g, f).start()

            @pl.when(g != me)
            def _():
                send_out(g, f).start()

    prepare(0)

    def one_round(t, carry):
        for f in range(per):

            @pl.when(has_below)
            def _():
                go_up(t, f).wait_recv()

            @pl.when(jnp.logical_not(has_below))
            def _():
                low_halo[t, f] = jnp.zeros(low_halo.shape[2:], jnp.float32)

            @pl.when(has_above)
            def _():
                go_down(t, f).wait_recv()

            @pl.when(jnp.logical_not(has_above))
            def _():
                high_halo[t, f] = jnp.zeros(high_halo.shape[2:], jnp.float32)

            advance(t, f)

        @pl.when(t + 1 < rounds)
        def _():
            prepare(t + 1)

        return carry

    lax.fori_loop(0, rounds, one_round, 0)

    def drain(t, carry):
        for f in range(per):

            @pl.when(has_above)
            def _():
                go_up(t, f).wait_send()

            @pl.when(has_below)
            def _():
                go_down(t, f).wait_send()

        return carry

    lax.fori_loop(0, rounds, drain, 0)
    for r in range(spans):
        for by in range(1, n_span):
            give_pack(r, by).wait_send()

    def finish(g, carry):
        for f in range(per):

            @pl.when(g == me)
            def _():
                keep_out(g, f).wait()

            @pl.when(g != me)
            def _():
                send_out(g, f).wait_send()
                got_out(g, f).wait_recv()

        return carry

    lax.fori_loop(0, n_span, finish, 0)


def packed(coupling, impulse, amplifier, nonlinear):
    spans, steps, _, channels, _ = coupling.shape
    rows = padded_rows(channels)
    taps = impulse.shape[-1]
    gains = jnp.broadcast_to(amplifier[:, None, :, None], (spans, steps, channels, 1))
    rates = jnp.broadcast_to(nonlinear[:, :, None, None], (spans, steps, channels, 1))
    gap = jnp.zeros((spans, steps, channels, LANES - 2 - channels), jnp.float32)
    tail = jnp.zeros((spans, steps, channels, LANES - channels), jnp.float32)
    body = jnp.concatenate(
        [coupling[:, :, 0], gap, rates, gains, coupling[:, :, 1], tail], axis=-1
    )
    body = jnp.pad(body, ((0, 0), (0, 0), (0, rows - channels), (0, 0)))
    lines = jnp.concatenate(
        [
            impulse[..., :1],
            jnp.zeros(impulse.shape[:-1] + (2 * LANES - taps,), jnp.float32),
            impulse[..., :0:-1],
        ],
        axis=-1,
    )
    lines = jnp.pad(lines, ((0, 0), (0, 0), (0, 6), (0, 0)))
    return jnp.concatenate([body, lines], axis=2)


def shards(launched, coupling, impulse, amplifier, nonlinear):
    n_span = lax.axis_size("span")
    n_tm = lax.axis_size("tm")
    frames, _, channels, samples = launched.shape
    _, spans, steps, _, taps = impulse.shape
    per = frames // n_span
    rows = padded_rows(channels)
    edge = steps * (taps - 1) // 2
    rounds = n_span * spans
    pack = packed(coupling[0], impulse[0], amplifier[0], nonlinear[0])
    sizes = (n_span, n_tm, spans, steps, channels, samples, per, edge)
    dma = pltpu.SemaphoreType.DMA
    return pl.pallas_call(
        functools.partial(kernel, sizes),
        out_shape=jax.ShapeDtypeStruct((1,) + launched.shape, jnp.float32),
        in_specs=[pl.BlockSpec(memory_space=pl.ANY)] * 2,
        out_specs=pl.BlockSpec(memory_space=pl.ANY),
        scratch_shapes=[
            pltpu.VMEM((per, 2, channels, samples), jnp.float32),
            pltpu.VMEM((rounds + 1, per, 2 * rows, samples), jnp.float32),
            pltpu.VMEM((rounds, per, 2 * rows, edge), jnp.float32),
            pltpu.VMEM((rounds, per, 2 * rows, edge), jnp.float32),
            pltpu.VMEM((n_span,) + pack.shape, jnp.float32),
            pltpu.VMEM((steps, 2 * rows, 2 * LANES), jnp.bfloat16),
            pltpu.VMEM((steps, 2 * rows, 2 * LANES), jnp.bfloat16),
            pltpu.VMEM((steps, 2 * LANES, 2 * LANES), jnp.bfloat16),
            pltpu.VMEM((steps, 2 * LANES, 2 * LANES), jnp.bfloat16),
            pltpu.VMEM((n_span, per, 2, channels, samples), jnp.float32),
            dma((per,)),
            dma((spans,)),
            dma((spans, n_span)),
            dma((n_span, spans)),
            dma((rounds, per)),
            dma((rounds, per)),
            dma((rounds, per)),
            dma((rounds, per)),
            dma((n_span, per)),
            dma((n_span, per)),
        ],
        compiler_params=pltpu.CompilerParams(
            collective_id=0, has_side_effects=True, vmem_limit_bytes=48 * 1024 * 1024
        ),
        name="link",
    )(launched, pack)


def solution(mesh):
    placed = (
        P(None, None, None, "tm"),
        P("span", None, None, None, None, None),
        P("span", None, None, None, None),
        P("span", None, None),
        P("span", None, None),
    )
    return jax.shard_map(
        shards,
        mesh=mesh,
        in_specs=placed,
        out_specs=P("span", None, None, None, "tm"),
        check_vma=False,
    )
```

time: 510 us -> 82.2 us (0.16); the launches traced: 502 us -> 82 us
  starting transfers between devices: 155 us -> 0 us
  waiting for transfers between devices: 97.5 us -> 0 us
  matrix products: 90.4 us -> 0 us
  local copies, waits for them, and re-layouts: 83.9 us -> 9.09 us
  Pallas kernels: 0 us -> 72.7 us
  other arithmetic: 54.1 us -> 0.05 us
  loops' own time: 20 us -> 0 us
    ppermute x55 -> x0, starting transfers between devices: 155 us -> none  [the longest x22 92.5 us: padded_2(): lax.ppermute(lax.slice_in_dim(block, 0, width, axis=dim), axis, backward)]
    ppermute x55 -> x0, waiting for transfers between devices: 97.5 us -> none  [the longest x11 66.2 us: passed_along(): return lax.ppermute(value, axis, pairs)]
    dot_general x88 -> x0, matrix products: 90.4 us -> none  [the longest x44 62.6 us: couple(): jnp.einsum('de,fel->fdl', mixer, flat, precision=lax.Precision.HIGHEST)]
    pallas_call x0 -> x1, Pallas kernels: none -> 72.7 us  [shards(): pl.pallas_call(functools.partial(kernel, sizes), out_shape=jax.ShapeDtype...]
    cos x44 -> x0, other arithmetic: 29.2 us -> none  [couple(): cosine = jnp.cos(phase)]
    slice x190 -> x2, local copies, waits for them, and re-layouts: 21.6 us -> 1.46 us  [the longest x1 0.77 us: packed(): impulse[..., :0:-1]]
    another operation x1 -> x0, loops' own time: 20 us -> none  [shards(): (_, stored), _ = lax.scan(advance, start, moments)]
    dynamic_slice x22 -> x0, local copies, waits for them, and re-layouts: 19.8 us -> none  [the longest x11 13.3 us: advance(): previous = lax.dynamic_index_in_dim(stored, position, 0, keepdims=True)]
  transfers between devices with their start and end apart: 55 -> 0, of which waited for: 44 -> 0; matrix products, arithmetic and copies ran while one was open for 3% -> 0% of each run, Pallas kernels for 0% -> 0%
where the time goes in v1:
time: 82.2 us; the launch traced here: 82 us
  Pallas kernels  72.7 us (88%)
  local copies, waits for them, and re-layouts  9.09 us (11%)
    pallas_call x1, Pallas kernels, shards(): pl.pallas_call(functools.partial(kernel, sizes), out_shape=jax.ShapeDtype...  72.7 us
    pallas_call x1, local copies, waits for them, and re-layouts, shards(): pl.pallas_call(functools.partial(kernel, sizes), out_shape=jax.ShapeDtype...  2.61 us

profile of v1, /device:TPU:23, one launch (start us, length us, event | category | flops | bytes accessed | tf_op | source)
XLA Modules:
  0.0 82.0 jit_solution(16866160206137375187)
XLA Ops:
  0.0 0.1 pad.13.clone
  0.1 0.8 slice.19
  0.8 0.1 rev.3
  0.9 0.7 slice.18
  1.6 0.8 broadcast_in_dim.27
  2.4 0.8 broadcast_in_dim.25
  3.2 1.1 %copy.10 = f32[1,2,2,2,110,110]{5,4,2,1,3,0:T(8,128)S(1)} copy(f32[1,2,2,2,110,110]{5,3,4,2,1,0:T(2,128)} %param.6) | data formatting | bytes 774400 | tf_op args[1]
  4.3 0.0 copy-start
  4.3 0.7 broadcast_in_dim.23
  5.0 1.3 %concatenate.9 = f32[2,2,110,256]{3,2,1,0:T(8,128)S(1)} concatenate(f32[2,2,110,110]{3,2,1,0:T(8,128)S(1)} %get-tuple-element.6, f32[2,2,110,16]{3,2,1,0:T(8,128)} %broadcast_in_dim.23, f32[2,2,110,1]{3,2,1,0:T(8,128)S(1)} %broadcast_in_dim.25, f32[2,2,110,1]{3,2,1,0:T(8,128)S(1)} %broadcast_in_dim.27, f32[2,2,110,110]{3,2,1,0:T(8,128)S(1)} %get-tuple-element.5, ...), dimensions={3} | concatenate | bytes 901120 | tf_op jit(solution)/shard_map/concatenate | solution.py:392
  6.4 0.0 copy-done
  6.4 0.2 copy.7.launched_ref
  6.6 72.7 %link.1 = f32[1,8,2,110,256]{4,3,2,1,0:T(8,128)S(1)} custom-call(f32[8,2,110,256]{3,2,1,0:T(8,128)S(1)} %copy.7.launched_ref, f32[2,2,120,256]{3,2,1,0:T(8,128)S(1)} %select_maximum_fusion.pack_ref), custom_call_target="tpu_custom_call" | custom-call | tf_op jit(solution)/shard_map/link/pallas_call | solution.py:420
  79.3 2.6 %copy.8 = f32[1,8,2,110,256]{4,2,3,1,0:T(2,128)} copy(f32[1,8,2,110,256]{4,3,2,1,0:T(8,128)S(1)} %link.1) | data formatting | bytes 3604480 | tf_op jit(solution)/shard_map/link/pallas_call | solution.py:420
  (5 shorter events, 0.1 us)
Async XLA Ops:
  4.3 2.1 %copy-start = (f32[8,2,110,256]{3,1,2,0:T(2,128)S(1)}, f32[8,2,110,256]{3,1,2,0:T(2,128)}, u32[]{:S(2)}) copy-start(f32[8,2,110,256]{3,1,2,0:T(2,128)} %param.5) | copy-start | bytes 5406724

commit v2 on v1

--- a/solution.py
+++ b/solution.py
@@ -21,11 +21,8 @@
     return high, low
 
 
-def product(a_high, a_low, b_high, b_low):
-    def dot(a, b):
-        return jnp.dot(a, b, preferred_element_type=jnp.float32)
-
-    return dot(a_high, b_high) + dot(a_low, b_high) + dot(a_high, b_low)
+def product(a, b):
+    return jnp.dot(a, b, preferred_element_type=jnp.float32)
 
 
 def cos_sin(angle):
@@ -48,22 +45,33 @@
 def kernel(
     sizes,
     launched_ref,
-    pack_ref,
+    coupling_ref,
+    impulse_ref,
+    amplifier_ref,
+    nonlinear_ref,
     out_ref,
     lstage,
+    taps_stage,
+    gain_stage,
+    rate_stage,
     own,
     low_halo,
     high_halo,
-    packs,
-    mix_high,
-    mix_low,
-    fir_high,
-    fir_low,
+    mixers,
+    smalls,
+    square,
+    mix,
+    fir,
     ostage,
     lsem,
-    psem,
-    pack_send,
-    pack_recv,
+    small_load,
+    own_mix,
+    small_send,
+    small_recv,
+    mix_send,
+    mix_recv,
+    share_send,
+    share_recv,
     up_send,
     up_recv,
     down_send,
@@ -73,6 +81,8 @@
 ):
     n_span, n_tm, spans, steps, channels, samples, per, edge = sizes
     rows = padded_rows(channels)
+    gain_row = 2 * spans * steps
+    rate_row = gain_row + spans
     rounds = n_span * spans
     me = lax.axis_index("span")
     tm = lax.axis_index("tm")
@@ -84,28 +94,93 @@
     def load(f):
         return pltpu.make_async_copy(launched_ref.at[me * per + f], lstage.at[f], lsem.at[f])
 
-    def own_pack(r):
-        return pltpu.make_async_copy(pack_ref.at[r], packs.at[me, r], psem.at[r])
-
-    def give_pack(r, by):
-        return pltpu.make_async_remote_copy(
-            src_ref=pack_ref.at[r],
-            dst_ref=packs.at[me, r],
-            send_sem=pack_send.at[r, by],
-            recv_sem=pack_recv.at[me, r],
+    core = lax.rem(tm, 2)
+    sibling = tm + 1 - 2 * core
+    small_loads = [
+        pltpu.make_async_copy(impulse_ref.at[0], taps_stage, small_load.at[0]),
+        pltpu.make_async_copy(amplifier_ref.at[0], gain_stage, small_load.at[1]),
+        pltpu.make_async_copy(nonlinear_ref.at[0], rate_stage, small_load.at[2]),
+    ]
+    own_mixers = pltpu.make_async_copy(coupling_ref.at[0], mixers.at[me], own_mix)
+
+    def give_small(by):
+        return pltpu.make_async_remote_copy(
+            src_ref=smalls.at[me],
+            dst_ref=smalls.at[me],
+            send_sem=small_send.at[by],
+            recv_sem=small_recv.at[me],
             device_id={"span": lax.rem(me + by, n_span)},
             device_id_type=MESH,
         )
 
-    def got_pack(g, r):
-        return pltpu.make_async_remote_copy(
-            src_ref=pack_ref.at[r],
-            dst_ref=packs.at[g, r],
-            send_sem=pack_send.at[r, 1],
-            recv_sem=pack_recv.at[g, r],
+    def got_small(g):
+        return pltpu.make_async_remote_copy(
+            src_ref=smalls.at[g],
+            dst_ref=smalls.at[g],
+            send_sem=small_send.at[1],
+            recv_sem=small_recv.at[g],
             device_id={"span": g},
             device_id_type=MESH,
         )
+
+    def give_mix(r, k, by):
+        return pltpu.make_async_remote_copy(
+            src_ref=coupling_ref.at[0, r, k, core],
+            dst_ref=mixers.at[me, r, k, core],
+            send_sem=mix_send.at[r, k, by],
+            recv_sem=mix_recv.at[me, r, k],
+            device_id={"span": lax.rem(me + by, n_span)},
+            device_id_type=MESH,
+        )
+
+    def got_mix(g, r, k):
+        return pltpu.make_async_remote_copy(
+            src_ref=coupling_ref.at[0, r, k, core],
+            dst_ref=mixers.at[g, r, k, core],
+            send_sem=mix_send.at[r, k, 1],
+            recv_sem=mix_recv.at[g, r, k],
+            device_id={"span": g},
+            device_id_type=MESH,
+        )
+
+    def share_mix(g, r, k):
+        return pltpu.make_async_remote_copy(
+            src_ref=mixers.at[g, r, k, core],
+            dst_ref=mixers.at[g, r, k, core],
+            send_sem=share_send.at[g, r, k],
+            recv_sem=share_recv.at[g, r, k],
+            device_id={"tm": sibling},
+            device_id_type=MESH,
+        )
+
+    def shared_mix(g, r, k):
+        return pltpu.make_async_remote_copy(
+            src_ref=mixers.at[g, r, k, 1 - core],
+            dst_ref=mixers.at[g, r, k, 1 - core],
+            send_sem=share_send.at[g, r, k],
+            recv_sem=share_recv.at[g, r, k],
+            device_id={"tm": sibling},
+            device_id_type=MESH,
+        )
+
+    def give(t):
+        r = t % spans
+
+        @pl.when(t // spans == me)
+        def _():
+            for k in range(steps):
+                for by in range(1, n_span):
+                    give_mix(r, k, by).start()
+
+    def relay(t):
+        g = t // spans
+        r = t % spans
+
+        @pl.when(g != me)
+        def _():
+            for k in range(steps):
+                got_mix(g, r, k).wait_recv()
+                share_mix(g, r, k).start()
 
     def go_up(t, f):
         return pltpu.make_async_remote_copy(
@@ -163,8 +238,9 @@
 
     for f in range(per):
         load(f).start()
-    for r in range(spans):
-        own_pack(r).start()
+    for copy in small_loads:
+        copy.start()
+    own_mixers.start()
 
     barrier = pltpu.get_barrier_semaphore()
     for by in range(1, n_span):
@@ -186,48 +262,76 @@
             own[0, f, pl.ds(part * rows + rows - 8, 8), :] = jnp.zeros((8, samples), jnp.float32)
             own[0, f, pl.ds(part * rows, channels), :] = lstage[f, part]
 
+    square[...] = jnp.zeros(square.shape, jnp.float32)
+    for copy in small_loads:
+        copy.wait()
+    smalls[me] = jnp.zeros(smalls.shape[1:], jnp.float32)
+    for r in range(spans):
+        for k in range(steps):
+            first = 2 * (r * steps + k)
+            smalls[me, pl.ds(first, 2), : taps_stage.shape[-1]] = taps_stage[r, k]
+    smalls[me, pl.ds(gain_row, spans), :channels] = gain_stage[...]
+    smalls[me, pl.ds(rate_row, spans), :steps] = rate_stage[...]
+
     pl.semaphore_wait(
         barrier,
         n_span - 1 + jnp.where(has_above, 1, 0) + jnp.where(has_below, 1, 0),
     )
-    for r in range(spans):
-        for by in range(1, n_span):
-            give_pack(r, by).start()
-        if r == 0:
-            for f in range(per):
-                send_edges(0, f)
-    for r in range(spans):
-        own_pack(r).wait()
+    give(0)
+    for f in range(per):
+        send_edges(0, f)
+    for by in range(1, n_span):
+        give_small(by).start()
+    own_mixers.wait()
+
+    def chosen(g, r, first):
+        both = smalls[g, pl.ds(first, spans)]
+        return jnp.sum(
+            jnp.where(lax.broadcasted_iota(jnp.int32, both.shape, 0) == r, both, 0.0),
+            axis=0,
+            keepdims=True,
+        )
 
     def prepare(t):
         g = t // spans
         r = t % spans
 
-        @pl.when(g != me)
-        def _():
-            got_pack(g, r).wait_recv()
+        @pl.when((g != me) & (r == 0))
+        def _():
+            got_small(g).wait_recv()
 
         for k in range(steps):
-            pack = packs[g, r, k]
-            real = pack[:rows, :LANES]
-            imag = pack[:rows, LANES:]
-            mixer = jnp.concatenate(
-                [
-                    jnp.concatenate([real, -imag], axis=1),
-                    jnp.concatenate([imag, real], axis=1),
-                ],
-                axis=0,
-            )
-            mix_high[k], mix_low[k] = halves(mixer)
+
+            @pl.when(g != me)
+            def _():
+                shared_mix(g, r, k).wait_recv()
+
+            real = mixers[g, r, k, 0]
+            imag = mixers[g, r, k, 1]
+            square[:channels, :channels] = real
+            square[:channels, pl.ds(LANES, channels)] = -imag
+            square[pl.ds(rows, channels), :channels] = imag
+            square[pl.ds(rows, channels), pl.ds(LANES, channels)] = real
+            high, low = halves(square[...])
+            mix[k, :, pl.ds(0, 2 * LANES)] = high
+            mix[k, :, pl.ds(2 * LANES, 2 * LANES)] = high
+            mix[k, :, pl.ds(4 * LANES, 2 * LANES)] = low
+            pair = smalls[g, pl.ds(0, gain_row)]
+            which = lax.broadcasted_iota(jnp.int32, pair.shape, 0)
             for part in range(2):
-                line = jnp.broadcast_to(pack[rows + part : rows + part + 1], (LANES, 2 * LANES))
+                line = jnp.sum(
+                    jnp.where(which == 2 * (r * steps + k) + part, pair, 0.0),
+                    axis=0,
+                    keepdims=True,
+                )
+                line = jnp.broadcast_to(line, (LANES, 2 * LANES))
                 band = pltpu.roll(line, 0, 1, stride=1, stride_axis=0)
                 column = pl.ds(part * LANES, LANES)
-                high, low = halves(band)
-                fir_high[k, pl.ds(0, LANES), column] = high[:, :LANES]
-                fir_high[k, pl.ds(LANES, LANES), column] = high[:, LANES:]
-                fir_low[k, pl.ds(0, LANES), column] = low[:, :LANES]
-                fir_low[k, pl.ds(LANES, LANES), column] = low[:, LANES:]
+                for half in range(2):
+                    high, low = halves(band[:, half * LANES : (half + 1) * LANES].T)
+                    fir[k, pl.ds(half * LANES, LANES), column] = high
+                    fir[k, pl.ds((2 + half) * LANES, LANES), column] = high
+                    fir[k, pl.ds((4 + half) * LANES, LANES), column] = low
 
     gap = jnp.zeros((LANES - rows, 1), jnp.bfloat16)
 
@@ -243,6 +347,9 @@
             + [own[t, f, :, pl.ds(i, LANES)] for i in range(0, samples, LANES)]
             + [high_halo[t, f, :, pl.ds(i, LANES)] for i in range(0, edge, LANES)]
         )
+        rates = chosen(g, r, rate_row)
+        gain = chosen(g, r, gain_row)[:, :LANES]
+        gain = jnp.broadcast_to(gain, (LANES, LANES)).T[:rows, :1]
         margin = edge
         for k in range(steps):
             margin = margin - edge // steps
@@ -262,7 +369,7 @@
                 ],
                 axis=0,
             )
-            wide = product(high, low, fir_high[k], fir_low[k])
+            wide = product(jnp.concatenate([high, low, high], axis=1), fir[k])
             real_parts = []
             imag_parts = []
             for b in range(count):
@@ -280,18 +387,16 @@
                 imag = imag * inside
             real_high, real_low = halves(real)
             imag_high, imag_low = halves(imag)
+            spread_high = spread(real_high, imag_high)
             mixed = product(
-                mix_high[k],
-                mix_low[k],
-                spread(real_high, imag_high),
-                spread(real_low, imag_low),
+                mix[k],
+                jnp.concatenate([spread_high, spread(real_low, imag_low), spread_high], axis=0),
             )
             power = jnp.sum(mixed * mixed, axis=0, keepdims=True)
-            cosine, sine = cos_sin(power * packs[g, r, k, 0:1, LANES - 2 : LANES - 1])
+            cosine, sine = cos_sin(power * rates[:, k : k + 1])
             real = mixed[:rows] * cosine - mixed[rows:] * sine
             imag = mixed[:rows] * sine + mixed[rows:] * cosine
             if k == steps - 1:
-                gain = packs[g, r, k, :rows, LANES - 1 : LANES]
                 real = real * gain
                 imag = imag * gain
             both = jnp.concatenate([real, imag], axis=0)
@@ -315,7 +420,9 @@
             def _():
                 send_out(g, f).start()
 
+    relay(0)
     prepare(0)
+    give(1)
 
     def one_round(t, carry):
         for f in range(per):
@@ -336,7 +443,18 @@
             def _():
                 high_halo[t, f] = jnp.zeros(high_halo.shape[2:], jnp.float32)
 
+            if f == 0:
+
+                @pl.when(t + 2 < rounds)
+                def _():
+                    give(t + 2)
+
             advance(t, f)
+            if f == 0:
+
+                @pl.when(t + 1 < rounds)
+                def _():
+                    relay(t + 1)
 
         @pl.when(t + 1 < rounds)
         def _():
@@ -360,9 +478,21 @@
         return carry
 
     lax.fori_loop(0, rounds, drain, 0)
-    for r in range(spans):
-        for by in range(1, n_span):
-            give_pack(r, by).wait_send()
+    for by in range(1, n_span):
+        give_small(by).wait_send()
+        for r in range(spans):
+            for k in range(steps):
+                give_mix(r, k, by).wait_send()
+
+    def drain_shares(t, carry):
+        @pl.when(t // spans != me)
+        def _():
+            for k in range(steps):
+                share_mix(t // spans, t % spans, k).wait_send()
+
+        return carry
+
+    lax.fori_loop(0, rounds, drain_shares, 0)
 
     def finish(g, carry):
         for f in range(per):
@@ -379,30 +509,6 @@
         return carry
 
     lax.fori_loop(0, n_span, finish, 0)
-
-
-def packed(coupling, impulse, amplifier, nonlinear):
-    spans, steps, _, channels, _ = coupling.shape
-    rows = padded_rows(channels)
-    taps = impulse.shape[-1]
-    gains = jnp.broadcast_to(amplifier[:, None, :, None], (spans, steps, channels, 1))
-    rates = jnp.broadcast_to(nonlinear[:, :, None, None], (spans, steps, channels, 1))
-    gap = jnp.zeros((spans, steps, channels, LANES - 2 - channels), jnp.float32)
-    tail = jnp.zeros((spans, steps, channels, LANES - channels), jnp.float32)
-    body = jnp.concatenate(
-        [coupling[:, :, 0], gap, rates, gains, coupling[:, :, 1], tail], axis=-1
-    )
-    body = jnp.pad(body, ((0, 0), (0, 0), (0, rows - channels), (0, 0)))
-    lines = jnp.concatenate(
-        [
-            impulse[..., :1],
-            jnp.zeros(impulse.shape[:-1] + (2 * LANES - taps,), jnp.float32),
-            impulse[..., :0:-1],
-        ],
-        axis=-1,
-    )
-    lines = jnp.pad(lines, ((0, 0), (0, 0), (0, 6), (0, 0)))
-    return jnp.concatenate([body, lines], axis=2)
 
 
 def shards(launched, coupling, impulse, amplifier, nonlinear):
@@ -414,29 +520,37 @@
     rows = padded_rows(channels)
     edge = steps * (taps - 1) // 2
     rounds = n_span * spans
-    pack = packed(coupling[0], impulse[0], amplifier[0], nonlinear[0])
+    small_rows = (2 * spans * steps + 2 * spans + 7) // 8 * 8
     sizes = (n_span, n_tm, spans, steps, channels, samples, per, edge)
     dma = pltpu.SemaphoreType.DMA
     return pl.pallas_call(
         functools.partial(kernel, sizes),
         out_shape=jax.ShapeDtypeStruct((1,) + launched.shape, jnp.float32),
-        in_specs=[pl.BlockSpec(memory_space=pl.ANY)] * 2,
+        in_specs=[pl.BlockSpec(memory_space=pl.ANY)] * 5,
         out_specs=pl.BlockSpec(memory_space=pl.ANY),
         scratch_shapes=[
             pltpu.VMEM((per, 2, channels, samples), jnp.float32),
+            pltpu.VMEM(impulse.shape[1:], jnp.float32),
+            pltpu.VMEM(amplifier.shape[1:], jnp.float32),
+            pltpu.VMEM(nonlinear.shape[1:], jnp.float32),
             pltpu.VMEM((rounds + 1, per, 2 * rows, samples), jnp.float32),
             pltpu.VMEM((rounds, per, 2 * rows, edge), jnp.float32),
             pltpu.VMEM((rounds, per, 2 * rows, edge), jnp.float32),
-            pltpu.VMEM((n_span,) + pack.shape, jnp.float32),
-            pltpu.VMEM((steps, 2 * rows, 2 * LANES), jnp.bfloat16),
-            pltpu.VMEM((steps, 2 * rows, 2 * LANES), jnp.bfloat16),
-            pltpu.VMEM((steps, 2 * LANES, 2 * LANES), jnp.bfloat16),
-            pltpu.VMEM((steps, 2 * LANES, 2 * LANES), jnp.bfloat16),
+            pltpu.VMEM((n_span,) + coupling.shape[1:], jnp.float32),
+            pltpu.VMEM((n_span, small_rows, 2 * LANES), jnp.float32),
+            pltpu.VMEM((2 * rows, 2 * LANES), jnp.float32),
+            pltpu.VMEM((steps, 2 * rows, 6 * LANES), jnp.bfloat16),
+            pltpu.VMEM((steps, 6 * LANES, 2 * LANES), jnp.bfloat16),
             pltpu.VMEM((n_span, per, 2, channels, samples), jnp.float32),
             dma((per,)),
-            dma((spans,)),
-            dma((spans, n_span)),
-            dma((n_span, spans)),
+            dma((3,)),
+            dma,
+            dma((n_span,)),
+            dma((n_span,)),
+            dma((spans, steps, n_span)),
+            dma((n_span, spans, steps)),
+            dma((n_span, spans, steps)),
+            dma((n_span, spans, steps)),
             dma((rounds, per)),
             dma((rounds, per)),
             dma((rounds, per)),
@@ -448,7 +562,7 @@
             collective_id=0, has_side_effects=True, vmem_limit_bytes=48 * 1024 * 1024
         ),
         name="link",
-    )(launched, pack)
+    )(launched, coupling, impulse, amplifier, nonlinear)
 
 
 def solution(mesh):

time: 82.2 us -> 93 us (1.13)
  Pallas kernels: 72.7 us -> 87.3 us
  local copies, waits for them, and re-layouts: 9.09 us -> 5.36 us
    pallas_call x1, Pallas kernels: 72.7 us -> 87.3 us  [shards(): pl.pallas_call(functools.partial(kernel, sizes), out_shape=jax.ShapeDtype...]
    broadcast_in_dim x5 -> x0, local copies, waits for them, and re-layouts: 2.26 us -> none  [the longest x1 0.77 us: packed(): jnp.broadcast_to(amplifier[:, None, :, None], (spans, steps, channels, 1))]
    unnamed x4 -> x8, local copies, waits for them, and re-layouts: 1.24 us -> 2.75 us
    slice x2 -> x0, local copies, waits for them, and re-layouts: 1.46 us -> none  [the longest x1 0.77 us: packed(): impulse[..., :0:-1]]
    concatenate x2 -> x0, local copies, waits for them, and re-layouts: 1.39 us -> none  [the longest x1 1.32 us: packed(): jnp.concatenate([coupling[:, :, 0], gap, rates, gains, coupling[:, :, 1],...]
where the time goes in v2:
time: 93 us; the launch traced here: 92.7 us
  Pallas kernels  87.3 us (94%)
  local copies, waits for them, and re-layouts  5.36 us (6%)
    pallas_call x1, Pallas kernels, shards(): pl.pallas_call(functools.partial(kernel, sizes), out_shape=jax.ShapeDtype...  87.3 us
    unnamed x8, local copies, waits for them, and re-layouts  2.75 us
    pallas_call x1, local copies, waits for them, and re-layouts, shards(): pl.pallas_call(functools.partial(kernel, sizes), out_shape=jax.ShapeDtype...  2.61 us

profile of v2, /device:TPU:23, one launch (start us, length us, event | category | flops | bytes accessed | tf_op | source)
XLA Modules:
  0.0 92.7 jit_solution(7093556571132911646)
XLA Ops:
  0.0 1.0 %copy.7.coupling_ref = f32[1,2,2,2,110,110]{5,4,3,2,1,0:T(8,128)S(1)} copy(f32[1,2,2,2,110,110]{5,3,4,2,1,0:T(2,128)} %param.6) | data formatting | bytes 774400 | tf_op args[1]
  1.1 0.0 copy-start
  1.1 0.0 copy-start.1
  1.1 0.0 copy-start.2
  1.1 1.7 %copy.6.launched_ref = f32[8,2,110,256]{3,2,1,0:T(8,128)S(1)} copy(f32[8,2,110,256]{3,1,2,0:T(2,128)} %param.5) | data formatting | bytes 3604480 | tf_op args[0]
  2.8 0.0 copy-done
  2.8 0.0 copy-done.1
  2.8 0.0 copy-done.2
  2.8 87.3 %link.1 = f32[1,8,2,110,256]{4,3,2,1,0:T(8,128)S(1)} custom-call(f32[8,2,110,256]{3,2,1,0:T(8,128)S(1)} %copy.6.launched_ref, f32[1,2,2,2,110,110]{5,4,3,2,1,0:T(8,128)S(1)} %copy.7.coupling_ref, f32[1,2,2,2,129]{4,3,2,1,0:T(2,128)S(1)} %copy-done, f32[1,2,110]{2,1,0:T(2,128)S(1)} %copy-done.1, f32[1,2,2]{2,1,0:T(2,128)S(1)} %copy-done.2), custom_call_target="tpu_custom_call" | custom-call | tf_op jit(solution)/shard_map/link/pallas_call | solution.py:526
  90.1 2.6 %copy.8 = f32[1,8,2,110,256]{4,2,3,1,0:T(2,128)} copy(f32[1,8,2,110,256]{4,3,2,1,0:T(8,128)S(1)} %link.1) | data formatting | bytes 3604480 | tf_op jit(solution)/shard_map/link/pallas_call | solution.py:526
Async XLA Ops:
  1.1 1.7 %copy-start = (f32[1,2,2,2,129]{4,3,2,1,0:T(2,128)S(1)}, f32[1,2,2,2,129]{4,3,2,1,0:T(2,128)}, u32[]{:S(2)}) copy-start(f32[1,2,2,2,129]{4,3,2,1,0:T(2,128)} %impulse_ref.1) | copy-start | bytes 12388
  1.1 1.7 %copy-start.1 = (f32[1,2,110]{2,1,0:T(2,128)S(1)}, f32[1,2,110]{2,1,0:T(2,128)}, u32[]{:S(2)}) copy-start(f32[1,2,110]{2,1,0:T(2,128)} %amplifier_ref.1) | copy-start | bytes 2644
  1.1 1.7 %copy-start.2 = (f32[1,2,2]{2,1,0:T(2,128)S(1)}, f32[1,2,2]{2,1,0:T(2,128)}, u32[]{:S(2)}) copy-start(f32[1,2,2]{2,1,0:T(2,128)} %nonlinear_ref.1) | copy-start | bytes 52

commit v3 on v2

--- a/solution.py
+++ b/solution.py
@@ -92,7 +92,7 @@
     has_above = tm < n_tm - 1
 
     def load(f):
-        return pltpu.make_async_copy(launched_ref.at[me * per + f], lstage.at[f], lsem.at[f])
+        return pltpu.make_async_copy(launched_ref.at[f], lstage.at[f], lsem.at[f])
 
     core = lax.rem(tm, 2)
     sibling = tm + 1 - 2 * core
@@ -339,90 +339,107 @@
         fill = jnp.broadcast_to(gap, (LANES - rows, real.shape[1]))
         return jnp.concatenate([real, fill, imag, fill], axis=0)
 
-    def advance(t, f):
+    def advance(t):
         g = t // spans
         r = t % spans
-        blocks = (
+        runs = [
             [low_halo[t, f, :, pl.ds(i, LANES)] for i in range(0, edge, LANES)]
             + [own[t, f, :, pl.ds(i, LANES)] for i in range(0, samples, LANES)]
             + [high_halo[t, f, :, pl.ds(i, LANES)] for i in range(0, edge, LANES)]
-        )
+            for f in range(per)
+        ]
         rates = chosen(g, r, rate_row)
         gain = chosen(g, r, gain_row)[:, :LANES]
-        gain = jnp.broadcast_to(gain, (LANES, LANES)).T[:rows, :1]
+        gain = jnp.broadcast_to(gain, (LANES, LANES)).T[:rows]
         margin = edge
         for k in range(steps):
             margin = margin - edge // steps
-            split = [halves(block) for block in blocks]
-            count = len(blocks) - 1
-            high = jnp.concatenate(
-                [
-                    jnp.concatenate([split[b][0], split[b + 1][0]], axis=1)
-                    for b in range(count)
-                ],
-                axis=0,
-            )
-            low = jnp.concatenate(
-                [
-                    jnp.concatenate([split[b][1], split[b + 1][1]], axis=1)
-                    for b in range(count)
-                ],
-                axis=0,
-            )
+            count = len(runs[0]) - 1
+            high = []
+            low = []
+            for run in runs:
+                split = [halves(block) for block in run]
+                for b in range(count):
+                    high.append(jnp.concatenate([split[b][0], split[b + 1][0]], axis=1))
+                    low.append(jnp.concatenate([split[b][1], split[b + 1][1]], axis=1))
+            high = jnp.concatenate(high, axis=0)
+            low = jnp.concatenate(low, axis=0)
             wide = product(jnp.concatenate([high, low, high], axis=1), fir[k])
-            real_parts = []
-            imag_parts = []
-            for b in range(count):
-                top = wide[b * 2 * rows : b * 2 * rows + rows]
-                bottom = wide[b * 2 * rows + rows : (b + 1) * 2 * rows]
-                real_parts.append(top[:, :LANES] - bottom[:, LANES:])
-                imag_parts.append(top[:, LANES:] + bottom[:, :LANES])
-            real = jnp.concatenate(real_parts, axis=1)
-            imag = jnp.concatenate(imag_parts, axis=1)
-            if margin > 0:
-                extent = count * LANES
-                place = tm * samples - margin + lax.broadcasted_iota(jnp.int32, (1, extent), 1)
-                inside = ((place >= 0) & (place < samples * n_tm)).astype(jnp.float32)
-                real = real * inside
-                imag = imag * inside
-            real_high, real_low = halves(real)
-            imag_high, imag_low = halves(imag)
-            spread_high = spread(real_high, imag_high)
+            spread_high = []
+            spread_low = []
+            for f in range(per):
+                for b in range(count):
+                    first = (f * count + b) * 2 * rows
+                    top = wide[first : first + rows]
+                    bottom = wide[first + rows : first + 2 * rows]
+                    real = top[:, :LANES] - bottom[:, LANES:]
+                    imag = top[:, LANES:] + bottom[:, :LANES]
+                    if b * LANES < margin or (b + 1) * LANES > margin + samples:
+                        place = (
+                            tm * samples
+                            - margin
+                            + b * LANES
+                            + lax.broadcasted_iota(jnp.int32, (1, LANES), 1)
+                        )
+                        inside = ((place >= 0) & (place < samples * n_tm)).astype(jnp.float32)
+                        real = real * inside
+                        imag = imag * inside
+                    real_high, real_low = halves(real)
+                    imag_high, imag_low = halves(imag)
+                    spread_high.append(spread(real_high, imag_high))
+                    spread_low.append(spread(real_low, imag_low))
+            spread_high = jnp.concatenate(spread_high, axis=1)
+            spread_low = jnp.concatenate(spread_low, axis=1)
             mixed = product(
-                mix[k],
-                jnp.concatenate([spread_high, spread(real_low, imag_low), spread_high], axis=0),
+                mix[k], jnp.concatenate([spread_high, spread_low, spread_high], axis=0)
             )
             power = jnp.sum(mixed * mixed, axis=0, keepdims=True)
             cosine, sine = cos_sin(power * rates[:, k : k + 1])
-            real = mixed[:rows] * cosine - mixed[rows:] * sine
-            imag = mixed[:rows] * sine + mixed[rows:] * cosine
-            if k == steps - 1:
-                real = real * gain
-                imag = imag * gain
-            both = jnp.concatenate([real, imag], axis=0)
-            blocks = [both[:, b * LANES : (b + 1) * LANES] for b in range(count)]
-        own[t + 1, f] = both
+            runs = []
+            for f in range(per):
+                run = []
+                for b in range(count):
+                    lanes = slice((f * count + b) * LANES, (f * count + b + 1) * LANES)
+                    real = mixed[:rows, lanes]
+                    imag = mixed[rows:, lanes]
+                    real, imag = (
+                        real * cosine[:, lanes] - imag * sine[:, lanes],
+                        real * sine[:, lanes] + imag * cosine[:, lanes],
+                    )
+                    if k == steps - 1:
+                        real = real * gain
+                        imag = imag * gain
+                    run.append(jnp.concatenate([real, imag], axis=0))
+                runs.append(run)
+        for f in range(per):
+            for b in range(count):
+                own[t + 1, f, :, pl.ds(b * LANES, LANES)] = runs[f][b]
 
         @pl.when(t + 1 < rounds)
         def _():
-            send_edges(t + 1, f)
+            for f in range(per):
+                send_edges(t + 1, f)
 
         @pl.when(r == spans - 1)
         def _():
-            ostage[g, f, 0] = real[:channels]
-            ostage[g, f, 1] = imag[:channels]
-
-            @pl.when(g == me)
-            def _():
-                keep_out(g, f).start()
-
-            @pl.when(g != me)
-            def _():
-                send_out(g, f).start()
+            for f in range(per):
+                for b in range(count):
+                    lanes = pl.ds(b * LANES, LANES)
+                    ostage[g, f, 0, :, lanes] = own[t + 1, f, pl.ds(0, channels), lanes]
+                    ostage[g, f, 1, :, lanes] = own[t + 1, f, pl.ds(rows, channels), lanes]
+
+                @pl.when(g == me)
+                def _():
+                    keep_out(g, f).start()
+
+                @pl.when(g != me)
+                def _():
+                    send_out(g, f).start()
 
     relay(0)
     prepare(0)
-    give(1)
+    for t in range(1, rounds):
+        give(t)
 
     def one_round(t, carry):
         for f in range(per):
@@ -443,18 +460,15 @@
             def _():
                 high_halo[t, f] = jnp.zeros(high_halo.shape[2:], jnp.float32)
 
-            if f == 0:
-
-                @pl.when(t + 2 < rounds)
-                def _():
-                    give(t + 2)
-
-            advance(t, f)
-            if f == 0:
-
-                @pl.when(t + 1 < rounds)
-                def _():
-                    relay(t + 1)
+        @pl.when((t > 0) & (t + 1 < rounds))
+        def _():
+            relay(t + 1)
+
+        advance(t)
+
+        @pl.when(t == 0)
+        def _():
+            relay(1)
 
         @pl.when(t + 1 < rounds)
         def _():
@@ -522,6 +536,7 @@
     rounds = n_span * spans
     small_rows = (2 * spans * steps + 2 * spans + 7) // 8 * 8
     sizes = (n_span, n_tm, spans, steps, channels, samples, per, edge)
+    mine = lax.dynamic_slice_in_dim(launched, lax.axis_index("span") * per, per, 0)
     dma = pltpu.SemaphoreType.DMA
     return pl.pallas_call(
         functools.partial(kernel, sizes),
@@ -562,7 +577,7 @@
             collective_id=0, has_side_effects=True, vmem_limit_bytes=48 * 1024 * 1024
         ),
         name="link",
-    )(launched, coupling, impulse, amplifier, nonlinear)
+    )(mine, coupling, impulse, amplifier, nonlinear)
 
 
 def solution(mesh):

time: 93 us -> 92 us (0.989)
    unnamed x8 -> x12, local copies, waits for them, and re-layouts: 2.75 us -> 1.68 us
where the time goes in v3:
time: 92 us; the launch traced here: 91.9 us
  Pallas kernels  87.3 us (95%)
  local copies, waits for them, and re-layouts  4.44 us (5%)
    pallas_call x1, Pallas kernels, shards(): pl.pallas_call(functools.partial(kernel, sizes), out_shape=jax.ShapeDtype...  87.3 us
    pallas_call x1, local copies, waits for them, and re-layouts, shards(): pl.pallas_call(functools.partial(kernel, sizes), out_shape=jax.ShapeDtype...  2.61 us

profile of v3, /device:TPU:23, one launch (start us, length us, event | category | flops | bytes accessed | tf_op | source)
XLA Modules:
  0.0 91.9 jit_solution(13644310581590144303)
XLA Ops:
  0.0 0.0 copy-start
  0.0 0.0 copy-start.3
  0.0 0.0 copy-start.2
  0.0 0.0 copy-start.1
  0.0 0.0 copy-start.4
  0.0 1.6 %copy-done = f32[8,2,110,256]{3,1,2,0:T(2,128)S(1)} copy-done((f32[8,2,110,256]{3,1,2,0:T(2,128)S(1)}, f32[8,2,110,256]{3,1,2,0:T(2,128)}, u32[]{:S(2)}) %copy-start) | copy-done | bytes 1802264
  1.6 0.2 constant_dynamic-slice_fusion
  1.8 0.0 copy-done.4
  1.9 0.0 copy-done.3
  1.9 0.0 copy-done.2
  1.9 0.0 copy-done.1
  1.9 87.3 %link.1 = f32[1,8,2,110,256]{4,3,2,1,0:T(8,128)S(1)} custom-call(f32[2,2,110,256]{3,2,1,0:T(8,128)S(1)} %copy.9.launched_ref, f32[1,2,2,2,110,110]{5,4,3,2,1,0:T(8,128)S(1)} %copy.7.coupling_ref, f32[1,2,2,2,129]{4,3,2,1,0:T(2,128)S(1)} %copy-done.1, f32[1,2,110]{2,1,0:T(2,128)S(1)} %copy-done.2, f32[1,2,2]{2,1,0:T(2,128)S(1)} %copy-done.3), custom_call_target="tpu_custom_call" | custom-call | tf_op jit(solution)/shard_map/link/pallas_call | solution.py:541
  89.2 2.6 %copy.8 = f32[1,8,2,110,256]{4,2,3,1,0:T(2,128)} copy(f32[1,8,2,110,256]{4,3,2,1,0:T(8,128)S(1)} %link.1) | data formatting | bytes 3604480 | tf_op jit(solution)/shard_map/link/pallas_call | solution.py:541
  (2 shorter events, 0.1 us)
Async XLA Ops:
  0.0 1.6 %copy-start = (f32[8,2,110,256]{3,1,2,0:T(2,128)S(1)}, f32[8,2,110,256]{3,1,2,0:T(2,128)}, u32[]{:S(2)}) copy-start(f32[8,2,110,256]{3,1,2,0:T(2,128)} %param.5) | copy-start | bytes 5406724
  0.0 1.9 %copy-start.3 = (f32[1,2,2]{2,1,0:T(2,128)S(1)}, f32[1,2,2]{2,1,0:T(2,128)}, u32[]{:S(2)}) copy-start(f32[1,2,2]{2,1,0:T(2,128)} %nonlinear_ref.1) | copy-start | bytes 52
  0.0 1.9 %copy-start.2 = (f32[1,2,110]{2,1,0:T(2,128)S(1)}, f32[1,2,110]{2,1,0:T(2,128)}, u32[]{:S(2)}) copy-start(f32[1,2,110]{2,1,0:T(2,128)} %amplifier_ref.1) | copy-start | bytes 2644
  0.0 1.9 %copy-start.1 = (f32[1,2,2,2,129]{4,3,2,1,0:T(2,128)S(1)}, f32[1,2,2,2,129]{4,3,2,1,0:T(2,128)}, u32[]{:S(2)}) copy-start(f32[1,2,2,2,129]{4,3,2,1,0:T(2,128)} %impulse_ref.1) | copy-start | bytes 12388
  0.0 1.8 %copy-start.4 = (f32[1,2,2,2,110,110]{5,3,4,2,1,0:T(2,128)S(1)}, f32[1,2,2,2,110,110]{5,3,4,2,1,0:T(2,128)}, u32[]{:S(2)}) copy-start(f32[1,2,2,2,110,110]{5,3,4,2,1,0:T(2,128)} %param.6) | copy-start | bytes 1161604

commit v4 on v2

--- a/solution.py
+++ b/solution.py
@@ -21,8 +21,11 @@
     return high, low
 
 
-def product(a, b):
-    return jnp.dot(a, b, preferred_element_type=jnp.float32)
+def product(a_high, a_low, b_high, b_low):
+    def dot(a, b):
+        return jnp.dot(a, b, preferred_element_type=jnp.float32)
+
+    return dot(a_high, b_high) + dot(a_low, b_high) + dot(a_high, b_low)
 
 
 def cos_sin(angle):
@@ -92,7 +95,7 @@
     has_above = tm < n_tm - 1
 
     def load(f):
-        return pltpu.make_async_copy(launched_ref.at[me * per + f], lstage.at[f], lsem.at[f])
+        return pltpu.make_async_copy(launched_ref.at[f], lstage.at[f], lsem.at[f])
 
     core = lax.rem(tm, 2)
     sibling = tm + 1 - 2 * core
@@ -270,6 +273,15 @@
         for k in range(steps):
             first = 2 * (r * steps + k)
             smalls[me, pl.ds(first, 2), : taps_stage.shape[-1]] = taps_stage[r, k]
+    row = lax.broadcasted_iota(jnp.int32, (2 * LANES, 2 * LANES), 0)
+    column = lax.broadcasted_iota(jnp.int32, (2 * LANES, 2 * LANES), 1)
+    turned = jnp.where((row + column == 0) | (row + column == 2 * LANES), 1.0, 0.0)
+    smalls[me, :gain_row] = jnp.dot(
+        smalls[me, :gain_row],
+        turned,
+        precision=lax.Precision.HIGHEST,
+        preferred_element_type=jnp.float32,
+    )
     smalls[me, pl.ds(gain_row, spans), :channels] = gain_stage[...]
     smalls[me, pl.ds(rate_row, spans), :steps] = rate_stage[...]
 
@@ -313,9 +325,8 @@
             square[pl.ds(rows, channels), :channels] = imag
             square[pl.ds(rows, channels), pl.ds(LANES, channels)] = real
             high, low = halves(square[...])
-            mix[k, :, pl.ds(0, 2 * LANES)] = high
-            mix[k, :, pl.ds(2 * LANES, 2 * LANES)] = high
-            mix[k, :, pl.ds(4 * LANES, 2 * LANES)] = low
+            mix[0, k] = high
+            mix[1, k] = low
             pair = smalls[g, pl.ds(0, gain_row)]
             which = lax.broadcasted_iota(jnp.int32, pair.shape, 0)
             for part in range(2):
@@ -327,11 +338,11 @@
                 line = jnp.broadcast_to(line, (LANES, 2 * LANES))
                 band = pltpu.roll(line, 0, 1, stride=1, stride_axis=0)
                 column = pl.ds(part * LANES, LANES)
+                high, low = halves(band)
                 for half in range(2):
-                    high, low = halves(band[:, half * LANES : (half + 1) * LANES].T)
-                    fir[k, pl.ds(half * LANES, LANES), column] = high
-                    fir[k, pl.ds((2 + half) * LANES, LANES), column] = high
-                    fir[k, pl.ds((4 + half) * LANES, LANES), column] = low
+                    place = pl.ds(half * LANES, LANES)
+                    fir[0, k, place, column] = high[:, half * LANES : (half + 1) * LANES]
+                    fir[1, k, place, column] = low[:, half * LANES : (half + 1) * LANES]
 
     gap = jnp.zeros((LANES - rows, 1), jnp.bfloat16)
 
@@ -349,7 +360,8 @@
         )
         rates = chosen(g, r, rate_row)
         gain = chosen(g, r, gain_row)[:, :LANES]
-        gain = jnp.broadcast_to(gain, (LANES, LANES)).T[:rows, :1]
+        gain = jnp.broadcast_to(gain, (LANES, LANES)).T[:rows]
+        gain = jnp.concatenate([gain] * (samples // LANES), axis=1)
         margin = edge
         for k in range(steps):
             margin = margin - edge // steps
@@ -369,7 +381,7 @@
                 ],
                 axis=0,
             )
-            wide = product(jnp.concatenate([high, low, high], axis=1), fir[k])
+            wide = product(high, low, fir[0, k], fir[1, k])
             real_parts = []
             imag_parts = []
             for b in range(count):
@@ -387,10 +399,11 @@
                 imag = imag * inside
             real_high, real_low = halves(real)
             imag_high, imag_low = halves(imag)
-            spread_high = spread(real_high, imag_high)
             mixed = product(
-                mix[k],
-                jnp.concatenate([spread_high, spread(real_low, imag_low), spread_high], axis=0),
+                mix[0, k],
+                mix[1, k],
+                spread(real_high, imag_high),
+                spread(real_low, imag_low),
             )
             power = jnp.sum(mixed * mixed, axis=0, keepdims=True)
             cosine, sine = cos_sin(power * rates[:, k : k + 1])
@@ -422,7 +435,8 @@
 
     relay(0)
     prepare(0)
-    give(1)
+    for t in range(1, rounds):
+        give(t)
 
     def one_round(t, carry):
         for f in range(per):
@@ -442,12 +456,6 @@
             @pl.when(jnp.logical_not(has_above))
             def _():
                 high_halo[t, f] = jnp.zeros(high_halo.shape[2:], jnp.float32)
-
-            if f == 0:
-
-                @pl.when(t + 2 < rounds)
-                def _():
-                    give(t + 2)
 
             advance(t, f)
             if f == 0:
@@ -522,6 +530,7 @@
     rounds = n_span * spans
     small_rows = (2 * spans * steps + 2 * spans + 7) // 8 * 8
     sizes = (n_span, n_tm, spans, steps, channels, samples, per, edge)
+    mine = lax.dynamic_slice_in_dim(launched, lax.axis_index("span") * per, per, 0)
     dma = pltpu.SemaphoreType.DMA
     return pl.pallas_call(
         functools.partial(kernel, sizes),
@@ -539,8 +548,8 @@
             pltpu.VMEM((n_span,) + coupling.shape[1:], jnp.float32),
             pltpu.VMEM((n_span, small_rows, 2 * LANES), jnp.float32),
             pltpu.VMEM((2 * rows, 2 * LANES), jnp.float32),
-            pltpu.VMEM((steps, 2 * rows, 6 * LANES), jnp.bfloat16),
-            pltpu.VMEM((steps, 6 * LANES, 2 * LANES), jnp.bfloat16),
+            pltpu.VMEM((2, steps, 2 * rows, 2 * LANES), jnp.bfloat16),
+            pltpu.VMEM((2, steps, 2 * LANES, 2 * LANES), jnp.bfloat16),
             pltpu.VMEM((n_span, per, 2, channels, samples), jnp.float32),
             dma((per,)),
             dma((3,)),
@@ -562,7 +571,7 @@
             collective_id=0, has_side_effects=True, vmem_limit_bytes=48 * 1024 * 1024
         ),
         name="link",
-    )(launched, coupling, impulse, amplifier, nonlinear)
+    )(mine, coupling, impulse, amplifier, nonlinear)
 
 
 def solution(mesh):

time: 93 us -> 77.6 us (0.83)
  Pallas kernels: 87.3 us -> 73 us
    pallas_call x1, Pallas kernels: 87.3 us -> 73 us  [shards(): pl.pallas_call(functools.partial(kernel, sizes), out_shape=jax.ShapeDtype...]
    unnamed x8 -> x12, local copies, waits for them, and re-layouts: 2.75 us -> 1.68 us
where the time goes in v4:
time: 77.6 us; the launch traced here: 77.5 us
  Pallas kernels  73 us (94%)
  local copies, waits for them, and re-layouts  4.44 us (6%)
    pallas_call x1, Pallas kernels, shards(): pl.pallas_call(functools.partial(kernel, sizes), out_shape=jax.ShapeDtype...  73 us
    pallas_call x1, local copies, waits for them, and re-layouts, shards(): pl.pallas_call(functools.partial(kernel, sizes), out_shape=jax.ShapeDtype...  2.61 us
    unnamed x12, local copies, waits for them, and re-layouts  1.68 us

profile of v4, /device:TPU:23, one launch (start us, length us, event | category | flops | bytes accessed | tf_op | source)
XLA Modules:
  0.0 77.5 jit_solution(5057821724859842375)
XLA Ops:
  0.0 0.0 copy-start
  0.0 0.0 copy-start.3
  0.0 0.0 copy-start.2
  0.0 0.0 copy-start.1
  0.0 0.0 copy-start.4
  0.0 1.6 %copy-done = f32[8,2,110,256]{3,1,2,0:T(2,128)S(1)} copy-done((f32[8,2,110,256]{3,1,2,0:T(2,128)S(1)}, f32[8,2,110,256]{3,1,2,0:T(2,128)}, u32[]{:S(2)}) %copy-start) | copy-done | bytes 1802264
  1.6 0.2 constant_dynamic-slice_fusion
  1.8 0.0 copy-done.4
  1.9 0.0 copy-done.3
  1.9 0.0 copy-done.2
  1.9 0.0 copy-done.1
  1.9 73.0 %link.1 = f32[1,8,2,110,256]{4,3,2,1,0:T(8,128)S(1)} custom-call(f32[2,2,110,256]{3,2,1,0:T(8,128)S(1)} %copy.9.launched_ref, f32[1,2,2,2,110,110]{5,4,3,2,1,0:T(8,128)S(1)} %copy.7.coupling_ref, f32[1,2,2,2,129]{4,3,2,1,0:T(2,128)S(1)} %copy-done.1, f32[1,2,110]{2,1,0:T(2,128)S(1)} %copy-done.2, f32[1,2,2]{2,1,0:T(2,128)S(1)} %copy-done.3), custom_call_target="tpu_custom_call" | custom-call | tf_op jit(solution)/shard_map/link/pallas_call | solution.py:535
  74.9 2.6 %copy.8 = f32[1,8,2,110,256]{4,2,3,1,0:T(2,128)} copy(f32[1,8,2,110,256]{4,3,2,1,0:T(8,128)S(1)} %link.1) | data formatting | bytes 3604480 | tf_op jit(solution)/shard_map/link/pallas_call | solution.py:535
  (2 shorter events, 0.1 us)
Async XLA Ops:
  0.0 1.6 %copy-start = (f32[8,2,110,256]{3,1,2,0:T(2,128)S(1)}, f32[8,2,110,256]{3,1,2,0:T(2,128)}, u32[]{:S(2)}) copy-start(f32[8,2,110,256]{3,1,2,0:T(2,128)} %param.5) | copy-start | bytes 5406724
  0.0 1.9 %copy-start.3 = (f32[1,2,2]{2,1,0:T(2,128)S(1)}, f32[1,2,2]{2,1,0:T(2,128)}, u32[]{:S(2)}) copy-start(f32[1,2,2]{2,1,0:T(2,128)} %nonlinear_ref.1) | copy-start | bytes 52
  0.0 1.9 %copy-start.2 = (f32[1,2,110]{2,1,0:T(2,128)S(1)}, f32[1,2,110]{2,1,0:T(2,128)}, u32[]{:S(2)}) copy-start(f32[1,2,110]{2,1,0:T(2,128)} %amplifier_ref.1) | copy-start | bytes 2644
  0.0 1.9 %copy-start.1 = (f32[1,2,2,2,129]{4,3,2,1,0:T(2,128)S(1)}, f32[1,2,2,2,129]{4,3,2,1,0:T(2,128)}, u32[]{:S(2)}) copy-start(f32[1,2,2,2,129]{4,3,2,1,0:T(2,128)} %impulse_ref.1) | copy-start | bytes 12388
  0.0 1.8 %copy-start.4 = (f32[1,2,2,2,110,110]{5,3,4,2,1,0:T(2,128)S(1)}, f32[1,2,2,2,110,110]{5,3,4,2,1,0:T(2,128)}, u32[]{:S(2)}) copy-start(f32[1,2,2,2,110,110]{5,3,4,2,1,0:T(2,128)} %param.6) | copy-start | bytes 1161604

commit v5 on v4

--- a/solution.py
+++ b/solution.py
@@ -367,28 +367,17 @@
             margin = margin - edge // steps
             split = [halves(block) for block in blocks]
             count = len(blocks) - 1
-            high = jnp.concatenate(
-                [
-                    jnp.concatenate([split[b][0], split[b + 1][0]], axis=1)
-                    for b in range(count)
-                ],
-                axis=0,
-            )
-            low = jnp.concatenate(
-                [
-                    jnp.concatenate([split[b][1], split[b + 1][1]], axis=1)
-                    for b in range(count)
-                ],
-                axis=0,
-            )
-            wide = product(high, low, fir[0, k], fir[1, k])
             real_parts = []
             imag_parts = []
             for b in range(count):
-                top = wide[b * 2 * rows : b * 2 * rows + rows]
-                bottom = wide[b * 2 * rows + rows : (b + 1) * 2 * rows]
-                real_parts.append(top[:, :LANES] - bottom[:, LANES:])
-                imag_parts.append(top[:, LANES:] + bottom[:, :LANES])
+                wide = product(
+                    jnp.concatenate([split[b][0], split[b + 1][0]], axis=1),
+                    jnp.concatenate([split[b][1], split[b + 1][1]], axis=1),
+                    fir[0, k],
+                    fir[1, k],
+                )
+                real_parts.append(wide[:rows, :LANES] - wide[rows:, LANES:])
+                imag_parts.append(wide[:rows, LANES:] + wide[rows:, :LANES])
             real = jnp.concatenate(real_parts, axis=1)
             imag = jnp.concatenate(imag_parts, axis=1)
             if margin > 0:

time: 77.6 us -> 76.5 us (0.986)
  Pallas kernels: 73 us -> 71.8 us
    pallas_call x1, Pallas kernels: 73 us -> 71.8 us  [shards(): pl.pallas_call(functools.partial(kernel, sizes), out_shape=jax.ShapeDtype...]
where the time goes in v5:
time: 76.5 us; the launch traced here: 76.3 us
  Pallas kernels  71.8 us (94%)
  local copies, waits for them, and re-layouts  4.44 us (6%)
    pallas_call x1, Pallas kernels, shards(): pl.pallas_call(functools.partial(kernel, sizes), out_shape=jax.ShapeDtype...  71.8 us
    pallas_call x1, local copies, waits for them, and re-layouts, shards(): pl.pallas_call(functools.partial(kernel, sizes), out_shape=jax.ShapeDtype...  2.61 us
    unnamed x12, local copies, waits for them, and re-layouts  1.68 us

profile of v5, /device:TPU:23, one launch (start us, length us, event | category | flops | bytes accessed | tf_op | source)
XLA Modules:
  0.0 76.3 jit_solution(11326767196595079687)
XLA Ops:
  0.0 0.0 copy-start
  0.0 0.0 copy-start.3
  0.0 0.0 copy-start.2
  0.0 0.0 copy-start.1
  0.0 0.0 copy-start.4
  0.0 1.6 %copy-done = f32[8,2,110,256]{3,1,2,0:T(2,128)S(1)} copy-done((f32[8,2,110,256]{3,1,2,0:T(2,128)S(1)}, f32[8,2,110,256]{3,1,2,0:T(2,128)}, u32[]{:S(2)}) %copy-start) | copy-done | bytes 1802264
  1.6 0.2 constant_dynamic-slice_fusion
  1.8 0.0 copy-done.4
  1.9 0.0 copy-done.3
  1.9 0.0 copy-done.2
  1.9 0.0 copy-done.1
  1.9 71.8 %link.1 = f32[1,8,2,110,256]{4,3,2,1,0:T(8,128)S(1)} custom-call(f32[2,2,110,256]{3,2,1,0:T(8,128)S(1)} %copy.9.launched_ref, f32[1,2,2,2,110,110]{5,4,3,2,1,0:T(8,128)S(1)} %copy.7.coupling_ref, f32[1,2,2,2,129]{4,3,2,1,0:T(2,128)S(1)} %copy-done.1, f32[1,2,110]{2,1,0:T(2,128)S(1)} %copy-done.2, f32[1,2,2]{2,1,0:T(2,128)S(1)} %copy-done.3), custom_call_target="tpu_custom_call" | custom-call | tf_op jit(solution)/shard_map/link/pallas_call | solution.py:524
  73.7 2.6 %copy.8 = f32[1,8,2,110,256]{4,2,3,1,0:T(2,128)} copy(f32[1,8,2,110,256]{4,3,2,1,0:T(8,128)S(1)} %link.1) | data formatting | bytes 3604480 | tf_op jit(solution)/shard_map/link/pallas_call | solution.py:524
  (2 shorter events, 0.1 us)
Async XLA Ops:
  0.0 1.6 %copy-start = (f32[8,2,110,256]{3,1,2,0:T(2,128)S(1)}, f32[8,2,110,256]{3,1,2,0:T(2,128)}, u32[]{:S(2)}) copy-start(f32[8,2,110,256]{3,1,2,0:T(2,128)} %param.5) | copy-start | bytes 5406724
  0.0 1.9 %copy-start.3 = (f32[1,2,2]{2,1,0:T(2,128)S(1)}, f32[1,2,2]{2,1,0:T(2,128)}, u32[]{:S(2)}) copy-start(f32[1,2,2]{2,1,0:T(2,128)} %nonlinear_ref.1) | copy-start | bytes 52
  0.0 1.9 %copy-start.2 = (f32[1,2,110]{2,1,0:T(2,128)S(1)}, f32[1,2,110]{2,1,0:T(2,128)}, u32[]{:S(2)}) copy-start(f32[1,2,110]{2,1,0:T(2,128)} %amplifier_ref.1) | copy-start | bytes 2644
  0.0 1.9 %copy-start.1 = (f32[1,2,2,2,129]{4,3,2,1,0:T(2,128)S(1)}, f32[1,2,2,2,129]{4,3,2,1,0:T(2,128)}, u32[]{:S(2)}) copy-start(f32[1,2,2,2,129]{4,3,2,1,0:T(2,128)} %impulse_ref.1) | copy-start | bytes 12388
  0.0 1.8 %copy-start.4 = (f32[1,2,2,2,110,110]{5,3,4,2,1,0:T(2,128)S(1)}, f32[1,2,2,2,110,110]{5,3,4,2,1,0:T(2,128)}, u32[]{:S(2)}) copy-start(f32[1,2,2,2,110,110]{5,3,4,2,1,0:T(2,128)} %param.6) | copy-start | bytes 1161604
